TPU v7x, 32 devices: a whole 2x2x4 slice. The times are simulated.
32 devices in a mesh: dp: 2 (over core), ctx: 8 (over z, x), tp: 2 (over y).
Axes of the slice: x: 2, y: 2, z: 4, core: 2. Of those that a mesh axis runs over, the one named last changes fastest.
Arguments:
- x_in: bfloat16 [2, 4096, 8192], P('dp', 'ctx', 'tp'), may hold values from -6 to 6
- grad_out: bfloat16 [2, 4096, 8192], P('dp', 'ctx', 'tp'), may hold values from -16 to 16
- state_maps: bfloat16 [2, 4096, 256], P('dp', 'ctx'), may hold values from -0.875 to 0.875
- dt_raw: float32 [2, 128, 4096], P('dp', 'tp', 'ctx'), may hold values from -3 to 20
- a_log: float32 [128], P('tp'), may hold values from -12 to 0
- saved_states: float32 [2, 8, 128, 64, 128], P('dp', 'ctx', 'tp'), may hold values from -0.625 to 0.625
- layer_in: bfloat16 [2, 4096, 8192], P('dp', 'ctx', 'tp'), may hold values from -40 to 40
- doc_lengths: int32 [2, 4], P('dp'), may hold values from 1 to 2048, 4096 in all within a row
Outputs:
- grad_x: bfloat16 [2, 4096, 8192], P('dp', 'ctx', 'tp')
- grad_maps: float32 [2, 4096, 256], P('dp', ('ctx', 'tp'))
- grad_dt_proj: float32 [128, 8192], P(('dp', 'ctx'), 'tp')
All inputs are finite; a program needn't handle non-finite values.
Results may differ from a plain program's by a relative error of at most 0.0055.
Values may be sent and summed in bfloat16 or wider, within the bound.
A program may use at most 128 MiB of HBM per device.

v0:
```python
import jax
import jax.numpy as jnp
from jax import lax
from jax.sharding import PartitionSpec as P

HEAD_DIM = 64
STATE = 128


head_group = 4
epsilon = 1e-06


def prefix(value, axis, join, neutral):
    count, mine = (lax.axis_size(axis), lax.axis_index(axis))
    pieces = jax.tree.map(lambda part: lax.all_gather(part, axis), value)
    pieces = jax.tree.map(lambda part: part[::-1], pieces)
    mine = count - 1 - mine
    subtotal = jax.tree.map(
        lambda part, zero: jnp.full_like(part, 0) + jnp.asarray(zero, part.dtype), value, neutral
    )

    def hop(position, subtotal):
        longer = join(subtotal, jax.tree.map(lambda part: part[position], pieces))
        return jax.tree.map(lambda new, old: jnp.where(position < mine, new, old), longer, subtotal)

    return lax.fori_loop(0, count - 1, hop, subtotal)


def segments(lengths_row, anchor, length):
    doc_ends = jnp.cumsum(lengths_row)
    positions = anchor + jnp.arange(length, dtype=jnp.int32)
    labels = jnp.sum((positions[:, None] >= doc_ends[None, :]).astype(jnp.int32), axis=1)
    before = jnp.sum((anchor - 1 >= doc_ends).astype(jnp.int32))
    before = jnp.where(anchor > 0, before, -1)
    return (labels, before)


def quad_terms(cumulative, step_sizes_delta, x_rows, dy_rows, pair_dot, causal):
    length, head_count, head_width = x_rows.shape

    def one_group(group_index, running):
        mixed_sum, r_local, dc_local = running
        offset = group_index * head_group
        c_part = lax.dynamic_slice_in_dim(cumulative, offset, head_group, 0)
        d_part = lax.dynamic_slice_in_dim(step_sizes_delta, offset, head_group, 0)
        x_part = lax.dynamic_slice_in_dim(x_rows, offset, head_group, 1)
        y_part = lax.dynamic_slice_in_dim(dy_rows, offset, head_group, 1)
        log_diffs = c_part[:, :, None] - c_part[:, None, :]
        kernel = jnp.where(causal[None], jnp.exp(jnp.where(causal[None], log_diffs, 0.0)), 0.0)
        weighted = kernel * pair_dot[None]
        rounded = weighted.astype(jnp.bfloat16)
        inner_dt = (
            jnp.einsum("ihp,jhp->hij", y_part, x_part, preferred_element_type=jnp.float32)
            * d_part[:, None, :]
        )
        r_part = jnp.einsum("hij,ihp->jhp", rounded, y_part, preferred_element_type=jnp.float32)
        products = weighted * inner_dt
        dc_part = jnp.sum(products, axis=2) - jnp.sum(products, axis=1)
        mixed_sum = mixed_sum + jnp.sum(kernel * inner_dt, axis=0)
        r_local = lax.dynamic_update_slice_in_dim(r_local, r_part, offset, 1)
        dc_local = lax.dynamic_update_slice_in_dim(dc_local, dc_part, offset, 0)
        return (mixed_sum, r_local, dc_local)

    initial = (
        jnp.zeros((length, length), jnp.float32),
        jnp.zeros((length, head_count, head_width), jnp.float32),
        jnp.zeros((head_count, length), jnp.float32),
    )
    return lax.fori_loop(0, head_count // head_group, one_group, initial)


def combine(earlier, later):
    return (earlier[0] * later[0], later[1] + later[0][:, None, None] * earlier[1])


def shards(x_in, grad_out, state_maps, dt_raw, a_log, saved_states, layer_in, doc_lengths):
    high = lax.Precision.HIGHEST
    length = x_in.shape[1]
    head_count = a_log.shape[0]
    x_rows = x_in[0].reshape(length, head_count, HEAD_DIM)
    dy_rows = grad_out[0].reshape(length, head_count, HEAD_DIM)
    b_half = state_maps[0, :, :STATE]
    c_half = state_maps[0, :, STATE:]
    raw_steps = dt_raw[0]
    states = saved_states[0, 0]
    anchor = lax.axis_index("ctx") * length
    labels, before = segments(doc_lengths[0], anchor, length)
    step_sizes_delta = jax.nn.softplus(raw_steps)
    decay_rate = -jnp.exp(a_log)
    cumulative = jnp.cumsum(decay_rate[:, None] * step_sizes_delta, axis=1)
    enter_w = jnp.exp(cumulative) * (labels == before).astype(jnp.float32)[None, :]
    leave_w = (
        jnp.exp(cumulative[:, -1:] - cumulative)
        * (labels == labels[-1]).astype(jnp.float32)[None, :]
    )
    scaled = (jnp.transpose(enter_w)[:, :, None] * dy_rows.astype(jnp.float32)).astype(jnp.bfloat16)
    local_grad = jnp.einsum("ihp,in->hpn", scaled, c_half, preferred_element_type=jnp.float32)
    decay_end = enter_w[:, -1]
    carried_all = prefix(
        (decay_end, local_grad),
        "ctx",
        combine,
        (jnp.ones_like(decay_end), jnp.zeros_like(local_grad)),
    )
    carried = carried_all[1]
    positions = jnp.arange(length)
    causal = (positions[:, None] >= positions[None, :]) & (labels[:, None] == labels[None, :])
    pair_dot = jnp.dot(c_half, b_half.T, preferred_element_type=jnp.float32)
    mixed_sum, r_local, dc_local = quad_terms(
        cumulative, step_sizes_delta, x_rows, dy_rows, pair_dot, causal
    )
    state_term = jnp.einsum(
        "ihp,hpn->in", scaled, states, precision=high, preferred_element_type=jnp.float32
    )
    local_b = jnp.einsum(
        "ij,in->jn", mixed_sum, c_half, precision=high, preferred_element_type=jnp.float32
    )
    local_c = (
        jnp.einsum(
            "ij,jn->in", mixed_sum, b_half, precision=high, preferred_element_type=jnp.float32
        )
        + state_term
    )
    state_c = jnp.einsum(
        "in,hpn->ihp", c_half, states, precision=high, preferred_element_type=jnp.float32
    )
    enter_out = enter_w * jnp.einsum(
        "ihp,ihp->hi", dy_rows, state_c, precision=high, preferred_element_type=jnp.float32
    )
    carry_b = jnp.einsum(
        "jn,hpn->jhp", b_half, carried, precision=high, preferred_element_type=jnp.float32
    )
    carry_r = jnp.transpose(leave_w)[:, :, None] * carry_b
    r_all = r_local + carry_r
    weighted_x = jnp.transpose(step_sizes_delta * leave_w)[:, :, None] * x_rows
    carry_bgrad = jnp.einsum(
        "jhp,hpn->jn", weighted_x, carried, precision=high, preferred_element_type=jnp.float32
    )
    grad_x = (jnp.transpose(step_sizes_delta)[:, :, None] * r_all).astype(jnp.bfloat16)
    w_term = step_sizes_delta * jnp.einsum(
        "jhp,jhp->hj", x_rows, carry_r, precision=high, preferred_element_type=jnp.float32
    )
    v_term = enter_w[:, -1] * jnp.sum(carried * states, axis=(1, 2))
    last_mask = (positions == length - 1).astype(jnp.float32)
    cum_grad = (
        dc_local
        + enter_out
        - w_term
        + (v_term + jnp.sum(w_term, axis=1))[:, None] * last_mask[None, :]
    )
    tail_sum = jnp.flip(jnp.cumsum(jnp.flip(cum_grad, 1), axis=1), 1)
    step_grad = (
        jnp.einsum("jhp,jhp->hj", x_rows, r_all, precision=high, preferred_element_type=jnp.float32)
        + decay_rate[:, None] * tail_sum
    )
    dt_grad = (step_grad * jax.nn.sigmoid(raw_steps)).astype(jnp.bfloat16)
    first_part = lax.psum_scatter(
        jnp.concatenate([local_b, local_c], axis=1).astype(jnp.bfloat16),
        "tp",
        scatter_dimension=0,
        tiled=True,
    ).astype(jnp.float32)
    second_part = lax.psum_scatter(carry_bgrad, "tp", scatter_dimension=0, tiled=True)
    grad_maps = jnp.concatenate(
        [first_part[:, :STATE] + second_part, first_part[:, STATE:]], axis=1
    )
    gathered = lax.all_gather(dt_grad, "tp", axis=0, tiled=True)
    tokens_in = layer_in[0]
    summed = lax.psum_scatter(
        jnp.dot(gathered, tokens_in, preferred_element_type=jnp.float32),
        ("dp", "ctx"),
        scatter_dimension=0,
        tiled=True,
    )
    squares = jnp.sum(summed * summed, axis=1)
    own_norm = jnp.sqrt(lax.psum(squares, "tp") + epsilon)
    target = lax.psum(jnp.sum(own_norm), ("dp", "ctx")) / gathered.shape[0]
    clip_scale = jnp.minimum(1.0, target / own_norm)
    grad_dt_proj = summed * clip_scale[:, None]
    return (grad_x.reshape(1, length, head_count * HEAD_DIM), grad_maps[None], grad_dt_proj)


def solution(mesh):
    in_specs = (
        P("dp", "ctx", "tp"),
        P("dp", "ctx", "tp"),
        P("dp", "ctx", None),
        P("dp", "tp", "ctx"),
        P("tp"),
        P("dp", "ctx", "tp", None, None),
        P("dp", "ctx", "tp"),
        P("dp", None),
    )
    out_specs = (P("dp", "ctx", "tp"), P("dp", ("ctx", "tp"), None), P(("dp", "ctx"), "tp"))
    return jax.shard_map(shards, mesh=mesh, in_specs=in_specs, out_specs=out_specs, check_vma=False)
```

profile of v0, /device:TPU:1, one launch (start us, length us, event | category | flops | bytes accessed | tf_op | source)
XLA Modules:
  0.0 452.8 jit_solution(7632388345502713044)
XLA Ops:
  17.2 6.4 %copy.129 = bf16[1,512,4096]{1,2,0:T(8,128)(2,1)} copy(bf16[1,512,4096]{2,1,0:T(8,128)(2,1)} %param.13) | data formatting | bytes 8388608 | tf_op args[1]
  23.7 3.1 fusion.27
  26.7 1.9 copy-done
  28.6 2.6 fusion.60
  32.3 6.4 %copy.130 = bf16[1,512,4096]{1,2,0:T(8,128)(2,1)} copy(bf16[1,512,4096]{2,1,0:T(8,128)(2,1)} %param.12) | data formatting | bytes 8388608 | tf_op args[0]
  40.0 5.2 %broadcast_in_dim.75 = f32[512,64,64]{0,2,1:T(8,128)} broadcast(f32[]{:T(128)} %constant.86.clone.1), dimensions={} | broadcast | bytes 8388612 | tf_op jit(solution)/shard_map/broadcast_in_dim | solution.py:67
  45.9 184.6 %while.32 = (s32[]{:T(128)}, f32[512,512]{1,0:T(8,128)S(1)}, f32[512,64,64]{0,2,1:T(8,128)}, f32[64,512]{1,0:T(8,128)}, f32[64,512]{1,0:T(8,128)S(1)}, /*index=5...) while((s32[]{:T(128)}, f32[512,512]{1,0:T(8,128)S(1)}, ...), condition=%wide.region_8.9_spmd.clone, body=%wide.region_4.8_spmd.clone.sunk | while | flops 285210624 | bytes 12701921 | solution.py:70
  47.0 3.7 fusion.96
  50.7 4.7 %fusion.95 = (f32[4,512]{1,0:T(4,128)S(1)}, f32[4,512]{1,0:T(4,128)S(1)}, f32[512,512]{1,0:T(8,128)}) fusion(f32[512,512]{1,0:T(8,128)S(1)} %copy-done.8, f32[4,512]{1,0:T(4,128)S(1)} %get-tuple-element.515, f32[4,512]{1,0:T(4,128)S(1)} %get-tuple-element.516, pred[512,512]{1,0:T(8,128)(4,1)S(1)} %fusion.94, ...), kind=kOutput, calls=%fused_computation.6.clone.1 | convolution fusion | flops 144437248 | bytes 2925568 | tf_op jit(solution)/shard_map/while/body/eval_jaxpr/ihp,jhp->hij/dot_general | solution.py:54
  58.5 3.7 fusion.96
  62.2 4.7 %fusion.95 = (f32[4,512]{1,0:T(4,128)S(1)}, f32[4,512]{1,0:T(4,128)S(1)}, f32[512,512]{1,0:T(8,128)}) fusion(f32[512,512]{1,0:T(8,128)S(1)} %copy-done.8, f32[4,512]{1,0:T(4,128)S(1)} %get-tuple-element.515, f32[4,512]{1,0:T(4,128)S(1)} %get-tuple-element.516, pred[512,512]{1,0:T(8,128)(4,1)S(1)} %fusion.94, ...), kind=kOutput, calls=%fused_computation.6.clone.1 | convolution fusion | flops 144437248 | bytes 2925568 | tf_op jit(solution)/shard_map/while/body/eval_jaxpr/ihp,jhp->hij/dot_general | solution.py:54
  70.0 3.7 fusion.96
  73.7 4.6 %fusion.95 = (f32[4,512]{1,0:T(4,128)S(1)}, f32[4,512]{1,0:T(4,128)S(1)}, f32[512,512]{1,0:T(8,128)}) fusion(f32[512,512]{1,0:T(8,128)S(1)} %copy-done.8, f32[4,512]{1,0:T(4,128)S(1)} %get-tuple-element.515, f32[4,512]{1,0:T(4,128)S(1)} %get-tuple-element.516, pred[512,512]{1,0:T(8,128)(4,1)S(1)} %fusion.94, ...), kind=kOutput, calls=%fused_computation.6.clone.1 | convolution fusion | flops 144437248 | bytes 2925568 | tf_op jit(solution)/shard_map/while/body/eval_jaxpr/ihp,jhp->hij/dot_general | solution.py:54
  81.6 3.7 fusion.96
  85.2 4.6 %fusion.95 = (f32[4,512]{1,0:T(4,128)S(1)}, f32[4,512]{1,0:T(4,128)S(1)}, f32[512,512]{1,0:T(8,128)}) fusion(f32[512,512]{1,0:T(8,128)S(1)} %copy-done.8, f32[4,512]{1,0:T(4,128)S(1)} %get-tuple-element.515, f32[4,512]{1,0:T(4,128)S(1)} %get-tuple-element.516, pred[512,512]{1,0:T(8,128)(4,1)S(1)} %fusion.94, ...), kind=kOutput, calls=%fused_computation.6.clone.1 | convolution fusion | flops 144437248 | bytes 2925568 | tf_op jit(solution)/shard_map/while/body/eval_jaxpr/ihp,jhp->hij/dot_general | solution.py:54
  93.1 3.7 fusion.96
  96.8 4.7 %fusion.95 = (f32[4,512]{1,0:T(4,128)S(1)}, f32[4,512]{1,0:T(4,128)S(1)}, f32[512,512]{1,0:T(8,128)}) fusion(f32[512,512]{1,0:T(8,128)S(1)} %copy-done.8, f32[4,512]{1,0:T(4,128)S(1)} %get-tuple-element.515, f32[4,512]{1,0:T(4,128)S(1)} %get-tuple-element.516, pred[512,512]{1,0:T(8,128)(4,1)S(1)} %fusion.94, ...), kind=kOutput, calls=%fused_computation.6.clone.1 | convolution fusion | flops 144437248 | bytes 2925568 | tf_op jit(solution)/shard_map/while/body/eval_jaxpr/ihp,jhp->hij/dot_general | solution.py:54
  104.6 3.7 fusion.96
  108.3 4.6 %fusion.95 = (f32[4,512]{1,0:T(4,128)S(1)}, f32[4,512]{1,0:T(4,128)S(1)}, f32[512,512]{1,0:T(8,128)}) fusion(f32[512,512]{1,0:T(8,128)S(1)} %copy-done.8, f32[4,512]{1,0:T(4,128)S(1)} %get-tuple-element.515, f32[4,512]{1,0:T(4,128)S(1)} %get-tuple-element.516, pred[512,512]{1,0:T(8,128)(4,1)S(1)} %fusion.94, ...), kind=kOutput, calls=%fused_computation.6.clone.1 | convolution fusion | flops 144437248 | bytes 2925568 | tf_op jit(solution)/shard_map/while/body/eval_jaxpr/ihp,jhp->hij/dot_general | solution.py:54
  116.1 3.7 fusion.96
  119.8 4.8 %fusion.95 = (f32[4,512]{1,0:T(4,128)S(1)}, f32[4,512]{1,0:T(4,128)S(1)}, f32[512,512]{1,0:T(8,128)}) fusion(f32[512,512]{1,0:T(8,128)S(1)} %copy-done.8, f32[4,512]{1,0:T(4,128)S(1)} %get-tuple-element.515, f32[4,512]{1,0:T(4,128)S(1)} %get-tuple-element.516, pred[512,512]{1,0:T(8,128)(4,1)S(1)} %fusion.94, ...), kind=kOutput, calls=%fused_computation.6.clone.1 | convolution fusion | flops 144437248 | bytes 2925568 | tf_op jit(solution)/shard_map/while/body/eval_jaxpr/ihp,jhp->hij/dot_general | solution.py:54
  127.8 3.7 fusion.96
  131.5 4.7 %fusion.95 = (f32[4,512]{1,0:T(4,128)S(1)}, f32[4,512]{1,0:T(4,128)S(1)}, f32[512,512]{1,0:T(8,128)}) fusion(f32[512,512]{1,0:T(8,128)S(1)} %copy-done.8, f32[4,512]{1,0:T(4,128)S(1)} %get-tuple-element.515, f32[4,512]{1,0:T(4,128)S(1)} %get-tuple-element.516, pred[512,512]{1,0:T(8,128)(4,1)S(1)} %fusion.94, ...), kind=kOutput, calls=%fused_computation.6.clone.1 | convolution fusion | flops 144437248 | bytes 2925568 | tf_op jit(solution)/shard_map/while/body/eval_jaxpr/ihp,jhp->hij/dot_general | solution.py:54
  139.3 3.7 fusion.96
  143.1 4.7 %fusion.95 = (f32[4,512]{1,0:T(4,128)S(1)}, f32[4,512]{1,0:T(4,128)S(1)}, f32[512,512]{1,0:T(8,128)}) fusion(f32[512,512]{1,0:T(8,128)S(1)} %copy-done.8, f32[4,512]{1,0:T(4,128)S(1)} %get-tuple-element.515, f32[4,512]{1,0:T(4,128)S(1)} %get-tuple-element.516, pred[512,512]{1,0:T(8,128)(4,1)S(1)} %fusion.94, ...), kind=kOutput, calls=%fused_computation.6.clone.1 | convolution fusion | flops 144437248 | bytes 2925568 | tf_op jit(solution)/shard_map/while/body/eval_jaxpr/ihp,jhp->hij/dot_general | solution.py:54
  150.9 3.7 fusion.96
  154.6 4.7 %fusion.95 = (f32[4,512]{1,0:T(4,128)S(1)}, f32[4,512]{1,0:T(4,128)S(1)}, f32[512,512]{1,0:T(8,128)}) fusion(f32[512,512]{1,0:T(8,128)S(1)} %copy-done.8, f32[4,512]{1,0:T(4,128)S(1)} %get-tuple-element.515, f32[4,512]{1,0:T(4,128)S(1)} %get-tuple-element.516, pred[512,512]{1,0:T(8,128)(4,1)S(1)} %fusion.94, ...), kind=kOutput, calls=%fused_computation.6.clone.1 | convolution fusion | flops 144437248 | bytes 2925568 | tf_op jit(solution)/shard_map/while/body/eval_jaxpr/ihp,jhp->hij/dot_general | solution.py:54
  162.4 3.7 fusion.96
  166.1 4.6 %fusion.95 = (f32[4,512]{1,0:T(4,128)S(1)}, f32[4,512]{1,0:T(4,128)S(1)}, f32[512,512]{1,0:T(8,128)}) fusion(f32[512,512]{1,0:T(8,128)S(1)} %copy-done.8, f32[4,512]{1,0:T(4,128)S(1)} %get-tuple-element.515, f32[4,512]{1,0:T(4,128)S(1)} %get-tuple-element.516, pred[512,512]{1,0:T(8,128)(4,1)S(1)} %fusion.94, ...), kind=kOutput, calls=%fused_computation.6.clone.1 | convolution fusion | flops 144437248 | bytes 2925568 | tf_op jit(solution)/shard_map/while/body/eval_jaxpr/ihp,jhp->hij/dot_general | solution.py:54
  173.9 3.7 fusion.96
  177.6 4.7 %fusion.95 = (f32[4,512]{1,0:T(4,128)S(1)}, f32[4,512]{1,0:T(4,128)S(1)}, f32[512,512]{1,0:T(8,128)}) fusion(f32[512,512]{1,0:T(8,128)S(1)} %copy-done.8, f32[4,512]{1,0:T(4,128)S(1)} %get-tuple-element.515, f32[4,512]{1,0:T(4,128)S(1)} %get-tuple-element.516, pred[512,512]{1,0:T(8,128)(4,1)S(1)} %fusion.94, ...), kind=kOutput, calls=%fused_computation.6.clone.1 | convolution fusion | flops 144437248 | bytes 2925568 | tf_op jit(solution)/shard_map/while/body/eval_jaxpr/ihp,jhp->hij/dot_general | solution.py:54
  185.4 3.7 fusion.96
  189.1 4.6 %fusion.95 = (f32[4,512]{1,0:T(4,128)S(1)}, f32[4,512]{1,0:T(4,128)S(1)}, f32[512,512]{1,0:T(8,128)}) fusion(f32[512,512]{1,0:T(8,128)S(1)} %copy-done.8, f32[4,512]{1,0:T(4,128)S(1)} %get-tuple-element.515, f32[4,512]{1,0:T(4,128)S(1)} %get-tuple-element.516, pred[512,512]{1,0:T(8,128)(4,1)S(1)} %fusion.94, ...), kind=kOutput, calls=%fused_computation.6.clone.1 | convolution fusion | flops 144437248 | bytes 2925568 | tf_op jit(solution)/shard_map/while/body/eval_jaxpr/ihp,jhp->hij/dot_general | solution.py:54
  196.9 3.7 fusion.96
  200.7 4.6 %fusion.95 = (f32[4,512]{1,0:T(4,128)S(1)}, f32[4,512]{1,0:T(4,128)S(1)}, f32[512,512]{1,0:T(8,128)}) fusion(f32[512,512]{1,0:T(8,128)S(1)} %copy-done.8, f32[4,512]{1,0:T(4,128)S(1)} %get-tuple-element.515, f32[4,512]{1,0:T(4,128)S(1)} %get-tuple-element.516, pred[512,512]{1,0:T(8,128)(4,1)S(1)} %fusion.94, ...), kind=kOutput, calls=%fused_computation.6.clone.1 | convolution fusion | flops 144437248 | bytes 2925568 | tf_op jit(solution)/shard_map/while/body/eval_jaxpr/ihp,jhp->hij/dot_general | solution.py:54
  208.5 3.7 fusion.96
  212.1 4.6 %fusion.95 = (f32[4,512]{1,0:T(4,128)S(1)}, f32[4,512]{1,0:T(4,128)S(1)}, f32[512,512]{1,0:T(8,128)}) fusion(f32[512,512]{1,0:T(8,128)S(1)} %copy-done.8, f32[4,512]{1,0:T(4,128)S(1)} %get-tuple-element.515, f32[4,512]{1,0:T(4,128)S(1)} %get-tuple-element.516, pred[512,512]{1,0:T(8,128)(4,1)S(1)} %fusion.94, ...), kind=kOutput, calls=%fused_computation.6.clone.1 | convolution fusion | flops 144437248 | bytes 2925568 | tf_op jit(solution)/shard_map/while/body/eval_jaxpr/ihp,jhp->hij/dot_general | solution.py:54
  220.0 3.7 fusion.96
  223.7 4.7 %fusion.95 = (f32[4,512]{1,0:T(4,128)S(1)}, f32[4,512]{1,0:T(4,128)S(1)}, f32[512,512]{1,0:T(8,128)}) fusion(f32[512,512]{1,0:T(8,128)S(1)} %copy-done.8, f32[4,512]{1,0:T(4,128)S(1)} %get-tuple-element.515, f32[4,512]{1,0:T(4,128)S(1)} %get-tuple-element.516, pred[512,512]{1,0:T(8,128)(4,1)S(1)} %fusion.94, ...), kind=kOutput, calls=%fused_computation.6.clone.1 | convolution fusion | flops 144437248 | bytes 2925568 | tf_op jit(solution)/shard_map/while/body/eval_jaxpr/ihp,jhp->hij/dot_general | solution.py:54
  232.1 4.4 fusion.39
  240.0 19.5 %all-reduce = f32[512]{0:T(512)S(1)} all-reduce(f32[512]{0:T(512)S(1)} %bitcast_dynamic-update-slice_fusion), channel_id=3, replica_groups=mesh['dp'=2,'ctx'=8,'tp'=2] {'ctx'}, use_global_device_ids=true, to_apply=%add | all-reduce | flops 512 | bytes 4096
  260.7 1.7 copy.140
  262.5 6.9 %multiply_reduce_fusion.1 = f32[64,512]{1,0:T(8,128)S(1)} fusion(bf16[64,512,64]{1,2,0:T(8,128)(2,1)} %bitcast.163, f32[1,1,64,64,128]{4,3,2,1,0:T(8,128)} %param.17, bf16[1,512,256]{2,1,0:T(8,128)(2,1)} %param.14), kind=kOutput, calls=%fused_computation.35 | convolution fusion | flops 3227484160 | bytes 6553600 | tf_op jit(solution)/shard_map/in,hpn->ihp/dot_general | solution.py:125
  271.0 11.8 %rev.13 = f32[8,64,64,128]{3,2,1,0:T(8,128)} reverse(f32[8,64,64,128]{3,2,1,0:T(8,128)} %bitcast.168), dimensions={0} | reverse | bytes 33554432 | tf_op jit(solution)/shard_map/rev | solution.py:17
  282.7 14.9 %while.33 = (s32[]{:T(128)}, f32[64,64,128]{2,1,0:T(8,128)S(1)}, s32[]{:T(128)}, f32[8,64,64,128]{3,2,1,0:T(8,128)}, f32[8,64]{1,0:T(8,128)S(1)}, /*index=5*/s32[]{:T(128)}, s32[]{:T(128)}) while((s32[]{:T(128)}, f32[64,64,128]{2,1,0:T(8,128)S(1)}, s32[]{:T(128)}, f32[8,64,64,128]{3,2,1,0:T(8,128)}, f32[8,64]{1,0:T(8,128)S(1)}, ...), condition=%wide.region_11.12_spmd.clone, body=%wide.region_10.11_spmd.clone.sunk | while | flops 2097156 | bytes 6292329 | solution.py:27
  282.7 2.1 fusion.97
  284.9 2.1 fusion.97
  287.0 2.1 fusion.97
  289.1 2.1 fusion.97
  291.3 2.1 fusion.97
  293.4 2.1 fusion.97
  295.5 2.1 fusion.97
  297.6 2.3 fusion.38
  300.4 9.8 %fusion.26 = (f32[64,512]{1,0:T(8,128)S(1)}, f32[64,512]{1,0:T(8,128)S(1)}, f32[64,64,512]{2,1,0:T(8,128)}) fusion(bf16[64,512,64]{1,2,0:T(8,128)(2,1)S(1)} %bitcast.167, f32[512,64]{0,1:T(8,128)S(1)} %copy.134, f32[512,64,64]{0,2,1:T(8,128)} %get-tuple-element.268, f32[64,64,128]{2,1,0:T(8,128)S(1)} %get-tuple-element.269, ...), kind=kOutput, calls=%fused_computation.31 | convolution fusion | flops 3235840000 | bytes 23592960 | tf_op jit(solution)/shard_map/jn,hpn->jhp/dot_general | solution.py:131
  310.6 1.9 multiply_add_fusion
  312.4 1.7 rev.15
  316.5 8.7 %fusion.42 = f32[512,128]{0,1:T(8,128)} fusion(f32[64,64,128]{2,1,0:T(8,128)S(1)} %get-tuple-element.269, bf16[512,64,64]{0,2,1:T(8,128)(2,1)} %get-tuple-element.593, f32[512,64]{0,1:T(8,128)S(1)} %copy-done.11), kind=kOutput, calls=%fused_computation.50 | convolution fusion | flops 3225419776 | bytes 6684672 | tf_op jit(solution)/shard_map/jhp,hpn->jn/dot_general | solution.py:137
  325.6 3.8 all_gather.15
  329.3 4.3 fusion.32
  335.6 10.7 %multiply_convert_fusion = bf16[512,64,64]{0,2,1:T(8,128)(2,1)} fusion(f32[512,64]{0,1:T(8,128)S(1)} %copy.122, f32[512,64,64]{0,2,1:T(8,128)} %get-tuple-element.268, f32[64,64,512]{2,1,0:T(8,128)} %get-tuple-element.422, f32[512,64]{0,1:T(8,128)S(1)} %copy.134), kind=kLoop, calls=%fused_computation.39 | loop fusion | flops 8388608 | bytes 21233664 | tf_op jit(solution)/shard_map/convert_element_type | solution.py:140
  346.3 6.4 %copy.145 = bf16[1,512,4096]{2,1,0:T(8,128)(2,1)} copy(bf16[1,512,4096]{1,2,0:T(8,128)(2,1)} %bitcast.169) | data formatting | bytes 8388608
  353.7 47.3 %reduce-scatter.8.cloned.1.call-done = f32[8,4096]{1,0:T(8,128)} async-done(((f32[128,4096]{1,0:T(8,128)}), f32[8,4096]{1,0:T(8,128)}) %reduce-scatter.8.cloned.1.call-update) | async-done | bytes 131088 | tf_op jit(solution)/shard_map/reduce_scatter | solution.py:170
  402.0 3.8 psum.14
  407.3 35.6 %psum.15 = f32[]{:T(128)} all-reduce(f32[]{:T(128)} %fusion.77), channel_id=1, replica_groups=mesh['dp'=2,'ctx'=8,'tp'=2] {'dp','ctx'}, use_global_device_ids=true, to_apply=%region_22.23 | all-reduce | flops 1 | bytes 8 | tf_op jit(solution)/shard_map/psum | solution.py:178
  (197 shorter events, 79.4 us)
Async XLA Ops:
  8.0 263.0 %all-gather.4.cloned.1.call-start = ((), (), s32[]{:S(2)}) async-start(), calls=%async_computation.6 | async-start | bytes 18874368 | tf_op jit(solution)/shard_map/all_gather | solution.py:16
  17.1 6.5 %copy-start.6 = (f32[64,512]{0,1:T(8,128)}, f32[64,512]{0,1:T(8,128)S(1)}, u32[]{:S(2)}) copy-start(f32[64,512]{0,1:T(8,128)S(1)} %get-tuple-element.419) | copy-start | bytes 393220
  23.7 5.0 %copy-start.3 = (bf16[1,512,256]{2,1,0:T(8,128)(2,1)S(1)}, bf16[1,512,256]{2,1,0:T(8,128)(2,1)}, u32[]{:S(2)}) copy-start(bf16[1,512,256]{2,1,0:T(8,128)(2,1)} %param.14) | copy-start | bytes 786436
  26.7 1.9 copy-start
  31.2 302.5 %reduce-scatter.4.cloned.1.call-start = ((), (), s32[]{:S(2)}) async-start(), calls=%async_computation.3 | async-start | bytes 393216 | tf_op jit(solution)/shard_map/reduce_scatter | solution.py:158
  45.9 186.2 %copy-start.2 = (f32[1,1,64,64,128]{4,3,2,1,0:T(8,128)S(1)}, f32[1,1,64,64,128]{4,3,2,1,0:T(8,128)}, u32[]{:S(2)}) copy-start(f32[1,1,64,64,128]{4,3,2,1,0:T(8,128)} %param.17) | copy-start | bytes 6291460
  47.0 3.7 copy-start.8
  58.5 3.7 copy-start.8
  70.0 3.7 copy-start.8
  81.5 3.7 copy-start.8
  93.1 3.7 copy-start.8
  104.6 3.7 copy-start.8
  116.1 3.7 copy-start.8
  127.8 3.7 copy-start.8
  139.3 3.7 copy-start.8
  150.9 3.7 copy-start.8
  162.4 3.7 copy-start.8
  173.9 3.7 copy-start.8
  185.4 3.7 copy-start.8
  196.9 3.7 copy-start.8
  208.5 3.7 copy-start.8
  220.0 3.7 copy-start.8
  230.5 5.9 %copy-start.4 = (bf16[1,512,256]{2,1,0:T(8,128)(2,1)S(1)}, bf16[1,512,256]{2,1,0:T(8,128)(2,1)}, u32[]{:S(2)}) copy-start(bf16[1,512,256]{2,1,0:T(8,128)(2,1)} %param.14) | copy-start | bytes 786436
  232.0 6.0 %copy-start.12 = (u32[32]{0:T(128)S(1)}, u32[32]{0:T(128)}, u32[]{:S(2)}) copy-start(u32[32]{0:T(128)} %constant.106) | copy-start | bytes 388
  237.9 114.8 %reduce-scatter.6.cloned.1.call-start = ((), (), s32[]{:S(2)}) async-start(), calls=%async_computation.4 | async-start | bytes 393216 | tf_op jit(solution)/shard_map/reduce_scatter | solution.py:164
  262.5 7.7 %copy-start.9 = (f32[512,64]{1,0:T(8,128)S(1)}, f32[512,64]{1,0:T(8,128)}, u32[]{:S(2)}) copy-start(f32[512,64]{1,0:T(8,128)} %get-tuple-element.414) | copy-start | bytes 393220
  282.7 17.2 %copy-start.5 = (bf16[1,512,256]{2,1,0:T(8,128)(2,1)S(1)}, bf16[1,512,256]{2,1,0:T(8,128)(2,1)}, u32[]{:S(2)}) copy-start(bf16[1,512,256]{2,1,0:T(8,128)(2,1)} %param.14) | copy-start | bytes 786436
  297.6 2.8 copy-start.1
  300.4 10.1 %copy-start.7 = (f32[64,512]{0,1:T(8,128)S(1)}, f32[64,512]{0,1:T(8,128)}, u32[]{:S(2)}) copy-start(f32[64,512]{0,1:T(8,128)} %copy-done.6) | copy-start | bytes 393220
  300.4 10.1 %copy-start.10 = (f32[64,512]{0,1:T(8,128)S(1)}, f32[64,512]{0,1:T(8,128)}, u32[]{:S(2)}) copy-start(f32[64,512]{0,1:T(8,128)} %copy.140) | copy-start | bytes 393220
  310.3 6.1 %copy-start.11 = (f32[512,64]{0,1:T(8,128)S(1)}, f32[512,64]{0,1:T(8,128)}, u32[]{:S(2)}) copy-start(f32[512,64]{0,1:T(8,128)} %copy.138) | copy-start | bytes 393220
  325.2 75.8 %reduce-scatter.8.cloned.1.call-start = ((), (), s32[]{:S(2)}) async-start(), calls=%async_computation.5 | async-start | bytes 2228224 | tf_op jit(solution)/shard_map/reduce_scatter | solution.py:170
Sparse Core Ops, SparseCore 0:
  31.4 229.5 all-gather.3
Sparse Core Ops, SparseCore 1:
  238.0 13.5 reduce-scatter.3
  325.3 12.2 reduce-scatter.5
  341.1 59.8 reduce-scatter.7
where the time goes:
time: 456 us; the launch traced here: 453 us
  matrix products  174 us (38%)
  other arithmetic  83.8 us (18%)
  local copies, waits for them, and re-layouts  65.8 us (14%)
  blocking collectives  62.8 us (14%)
  waiting for transfers between devices  47.4 us (10%)
  between operations  18 us (4%)
    dot_general x16, matrix products, one_group(): jnp.einsum('ihp,jhp->hij', y_part, x_part, preferred_element_type=jnp.flo...  74.6 us
    dot_general x16, matrix products, one_group(): jnp.einsum('hij,ihp->jhp', rounded, y_part, preferred_element_type=jnp.fl...  59.2 us
    reduce_scatter x1, waiting for transfers between devices, shards(): lax.psum_scatter(jnp.dot(gathered, tokens_in, preferred_element_type=jnp....  47.3 us
    psum x1, blocking collectives, shards(): target = lax.psum(jnp.sum(own_norm), ('dp', 'ctx')) / gathered.shape[0]  35.6 us
    unnamed x33, local copies, waits for them, and re-layouts  25.8 us
    add x16, other arithmetic, one_group(): mixed_sum = mixed_sum + jnp.sum(kernel * inner_dt, axis=0)  25.4 us
    unnamed x1, blocking collectives  19.5 us
    select_n x7, other arithmetic, hop(): jnp.where(position < mine, new, old)  14.6 us
  transfers between devices with their start and end apart: 4, of which 1 were waited for; matrix products, arithmetic and copies ran while one was open for 65% of the time, Pallas kernels for 0%

commit v1 on v0

v1 whole, which is shorter than its diff:
```python
import functools

import jax
import jax.numpy as jnp
from jax import lax
from jax.experimental import pallas as pl
from jax.experimental.pallas import tpu as pltpu
from jax.sharding import PartitionSpec as P

HEAD_DIM = 64
STATE = 128
PAIR = 2 * HEAD_DIM
TILE = 256
CHUNK = 64
epsilon = 1e-06
LOG2E = 1.4426950408889634
f32, bf16 = jnp.float32, jnp.bfloat16


def mm(a, b, ca, cb):
    return lax.dot_general(a, b, (((ca,), (cb,)), ((), ())), preferred_element_type=f32)


def spread(cols, first, second, rows):
    lane = lax.broadcasted_iota(jnp.int32, (rows, PAIR), 1)
    return jnp.where(lane < HEAD_DIM, cols[:, first : first + 1], cols[:, second : second + 1])


def head_sums(value, pair):
    high = value.astype(bf16)
    low = (value - high.astype(f32)).astype(bf16)
    row = lax.broadcasted_iota(jnp.int32, (2 * PAIR, 128), 0) % PAIR
    col = lax.broadcasted_iota(jnp.int32, (2 * PAIR, 128), 1)
    chosen = col == 2 * pair + jnp.where(row >= HEAD_DIM, 1, 0)
    return mm(jnp.concatenate([high, low], axis=1), jnp.where(chosen, 1.0, 0.0).astype(bf16), 1, 0)


def enter_kernel(pairs, aux_ref, dy_ref, c_ref, s_ref, local_ref, sterm_ref, eo_ref):
    step = pl.program_id(0)

    @pl.when(step == 0)
    def _():
        sterm_ref[...] = jnp.zeros_like(sterm_ref)
        eo_ref[...] = jnp.zeros_like(eo_ref)

    rows = dy_ref.shape[0]
    c_rows = c_ref[...]
    for p in range(pairs):
        at = slice(p * PAIR, (p + 1) * PAIR)
        cols = aux_ref[p].T
        wide = dy_ref[:, at].astype(f32) * spread(cols, 6, 7, rows)
        scaled = wide.astype(bf16)
        local_ref[at, :] = mm(scaled, c_rows, 0, 0).astype(bf16)
        state = s_ref[at, :].astype(bf16)
        sterm_ref[...] += mm(scaled, state, 1, 0)
        eo_ref[...] += head_sums(wide * mm(c_rows, state, 1, 1), step * pairs + p)


def quad_kernel(
    pairs, aux_ref, x_ref, dy_ref, b_ref, c_ref, labr_ref, labc_ref, *refs
):
    min_ref = refs[0] if len(refs) > 4 else None
    r_ref, a_ref, msum_ref, cb_ref = refs[-4:]
    length = x_ref.shape[0]

    @pl.when(pl.program_id(0) == 0)
    def _():
        at_j = lax.broadcasted_iota(jnp.int32, (length, length), 0)
        at_i = lax.broadcasted_iota(jnp.int32, (length, length), 1)
        keep = (at_i >= at_j) & (labc_ref[...] == labr_ref[...])
        cb_ref[...] = jnp.where(keep, mm(b_ref[...], c_ref[...], 1, 1), 0.0)
        msum_ref[...] = jnp.zeros_like(msum_ref) if min_ref is None else min_ref[...]

    blocks = length // TILE
    lane = lax.broadcasted_iota(jnp.int32, (length, PAIR), 1)
    for p in range(pairs):
        at = slice(p * PAIR, (p + 1) * PAIR)
        aux = aux_ref[p]
        cols = aux.T
        x = x_ref[:, at]
        dy = dy_ref[:, at]
        zero = jnp.zeros_like(dy)
        dys = (jnp.where(lane < HEAD_DIM, dy, zero), jnp.where(lane < HEAD_DIM, zero, dy))
        sums = [[jnp.zeros((8, TILE), f32) for _ in range(blocks)] for _ in range(2)]
        for jb in range(blocks):
            j0 = jb * TILE
            weights, sources = [], []
            for ib in range(jb, blocks):
                i0 = ib * TILE
                inner = [mm(x[j0 : j0 + TILE], dys[s][i0 : i0 + TILE], 1, 1) for s in range(2)]
                pieces = [[], []]
                for c in range(TILE // CHUNK):
                    lo = c * CHUNK
                    rows = slice(j0 + lo, j0 + lo + CHUNK)
                    cb = cb_ref[rows, i0 : i0 + TILE]
                    total = None
                    for s in range(2):
                        power = aux[s : s + 1, i0 : i0 + TILE] - cols[rows, 2 + s : 3 + s]
                        if ib == jb:
                            power = jnp.minimum(power, 16.0)
                        decay = jnp.exp2(power)
                        pieces[s].append((decay * cb).astype(bf16))
                        mixed = decay * inner[s][lo : lo + CHUNK]
                        total = mixed if total is None else total + mixed
                        product = (mixed * cb).reshape(CHUNK // 8, 8, TILE)
                        sums[s][ib] = sums[s][ib] + jnp.sum(product, axis=0)
                    msum_ref[rows, i0 : i0 + TILE] += total
                for s in range(2):
                    weights.append(jnp.concatenate(pieces[s], axis=0))
                    sources.append(dys[s][i0 : i0 + TILE])
            r_ref[j0 : j0 + TILE, at] = mm(
                jnp.concatenate(weights, axis=1), jnp.concatenate(sources, axis=0), 1, 0
            )
        for s in range(2):
            for ib in range(blocks):
                a_ref[0, 2 * p + s : 2 * p + s + 1, ib * TILE : (ib + 1) * TILE] = jnp.sum(
                    sums[s][ib], axis=0, keepdims=True
                )


def leave_kernel(
    pairs, aux_ref, x_ref, r_ref, b_ref, carry_ref, s_ref, gx_ref, u_ref, bgrad_ref, vw_ref
):
    step = pl.program_id(0)

    @pl.when(step == 0)
    def _():
        u_ref[...] = jnp.zeros_like(u_ref)
        bgrad_ref[...] = jnp.zeros_like(bgrad_ref)

    rows = x_ref.shape[0]
    for p in range(pairs):
        at = slice(p * PAIR, (p + 1) * PAIR)
        cols = aux_ref[p].T
        weight = spread(cols, 4, 5, rows)
        carry = carry_ref[at, :]
        x = x_ref[:, at].astype(f32)
        after = weight * mm(b_ref[...], carry, 1, 1)
        grad = r_ref[:, at] + after
        gx_ref[:, at] = grad.astype(bf16)
        u_ref[...] += head_sums(x * grad, step * pairs + p)
        bgrad_ref[...] += mm((weight * x).astype(bf16), carry, 1, 0)
        both = carry.astype(f32) * s_ref[at, :]
        vw_ref[p, 0:1, :] = jnp.sum(both[:HEAD_DIM], axis=0, keepdims=True)
        vw_ref[p, 1:2, :] = jnp.sum(both[HEAD_DIM:], axis=0, keepdims=True)
        vw_ref[p, 2:3, :] = jnp.sum(x * after, axis=0, keepdims=True)
        vw_ref[p, 3:8, :] = jnp.zeros((5, STATE), f32)


def segments(lengths_row, anchor, length):
    doc_ends = jnp.cumsum(lengths_row)
    positions = anchor + jnp.arange(length, dtype=jnp.int32)
    labels = jnp.sum((positions[:, None] >= doc_ends[None, :]).astype(jnp.int32), axis=1)
    before = jnp.sum((anchor - 1 >= doc_ends).astype(jnp.int32))
    before = jnp.where(anchor > 0, before, -1)
    return (labels, before)


def full(shape):
    return pl.BlockSpec(shape, lambda g: (0,) * len(shape))


def shift(value, back, count):
    if back >= count:
        return jax.tree.map(jnp.zeros_like, value)
    moves = [(k, k - back) for k in range(back, count)]
    return jax.tree.map(lambda part: lax.ppermute(part, "ctx", moves), value)


def shards(x_in, grad_out, state_maps, dt_raw, a_log, saved_states, layer_in, doc_lengths):
    high = lax.Precision.HIGHEST
    length, width = x_in.shape[1:]
    head_count = a_log.shape[0]
    pair_count = head_count // 2
    x_rows, dy_rows = x_in[0], grad_out[0]
    b_half = state_maps[0, :, :STATE]
    c_half = state_maps[0, :, STATE:]
    raw_steps = dt_raw[0]
    states = saved_states.reshape(width, STATE)
    count = lax.axis_size("ctx")
    anchor = lax.axis_index("ctx") * length
    labels, before = segments(doc_lengths[0], anchor, length)
    positions = jnp.arange(length)
    upto = (positions[:, None] <= positions[None, :]).astype(f32)
    steps = jax.nn.softplus(raw_steps)
    decay_rate = -jnp.exp(a_log)
    cumulative = jnp.dot(decay_rate[:, None] * steps, upto, precision=high)
    enter_w = jnp.exp(cumulative) * (labels == before).astype(f32)[None, :]
    leave_w = jnp.exp(cumulative[:, -1:] - cumulative) * (labels == labels[-1]).astype(f32)[None, :]
    scaled_cum = cumulative * LOG2E
    aux = jnp.stack([scaled_cum, scaled_cum - jnp.log2(steps), steps * leave_w, enter_w])
    aux = aux.reshape(4, pair_count, 2, length).transpose(1, 0, 2, 3)
    aux = aux.reshape(pair_count, 8, length)
    ends = enter_w[:, -1]

    wide_pairs = 4
    groups = pair_count // wide_pairs
    aux_spec = pl.BlockSpec((wide_pairs, 8, length), lambda g: (g, 0, 0))
    col_spec = pl.BlockSpec((length, wide_pairs * PAIR), lambda g: (0, g))
    row_spec = pl.BlockSpec((wide_pairs * PAIR, STATE), lambda g: (g, 0))
    limit = pltpu.CompilerParams(vmem_limit_bytes=40 * 1024 * 1024)
    local, state_term, enter_out = pl.pallas_call(
        functools.partial(enter_kernel, wide_pairs),
        grid=(groups,),
        in_specs=[aux_spec, col_spec, full((length, STATE)), row_spec],
        out_specs=[row_spec, full((length, STATE)), full((length, 128))],
        out_shape=[
            jax.ShapeDtypeStruct((width, STATE), bf16),
            jax.ShapeDtypeStruct((length, STATE), f32),
            jax.ShapeDtypeStruct((length, 128), f32),
        ],
        compiler_params=limit,
        name="enter",
    )(aux, dy_rows, c_half, states)

    odd = lax.axis_index("ctx") % 2
    half = head_count // 2
    swap = [(k, k ^ 1) for k in range(count)]

    def take(value, which):
        return lax.dynamic_index_in_dim(value, which, 0, keepdims=False)

    whole_local = local.reshape(2, half, HEAD_DIM * STATE)
    half_ends = ends.reshape(2, half)
    mine, mine_end = take(whole_local, odd), take(half_ends, odd)
    other = lax.ppermute(take(whole_local, 1 - odd), "ctx", swap)
    other_end = lax.ppermute(take(half_ends, 1 - odd), "ctx", swap)
    first = jnp.where(odd == 0, mine, other).astype(f32)
    second = jnp.where(odd == 0, other, mine).astype(f32)
    first_end = jnp.where(odd == 0, mine_end, other_end)
    group = (first + first_end[:, None] * second).astype(bf16)
    group_end = mine_end * other_end
    reach, window = 1, max(count // 4, 1)
    while reach < window:
        ahead, ahead_end = shift((group, group_end), 2 * reach, count)
        group = (group.astype(f32) + group_end[:, None] * ahead.astype(f32)).astype(bf16)
        group_end = group_end * ahead_end
        reach *= 2
    after = shift(group, 2, count)
    even_end = jnp.where(odd == 0, other_end, mine_end)
    even_after = (second + even_end[:, None] * after.astype(f32)).astype(bf16)
    back = lax.ppermute(jnp.where(odd == 0, after, even_after), "ctx", swap)
    kept = jnp.where(odd == 0, even_after, after)
    carry = jnp.where(odd == 0, jnp.stack([kept, back]), jnp.stack([back, kept]))
    carry = carry.reshape(width, STATE)

    quad_pairs = 2
    parts = 4 if pair_count % (4 * quad_pairs) == 0 else 1
    quad_groups = pair_count // quad_pairs // parts
    labr, labc = labels[None, :], labels[:, None]
    mixed = r_local = None
    a_parts = []
    for part in range(parts):
        base = part * quad_groups
        quad_spec = pl.BlockSpec((length, quad_pairs * PAIR), lambda g, base=base: (0, base + g))
        r_local, a_part, mixed = pl.pallas_call(
            functools.partial(quad_kernel, quad_pairs),
            grid=(quad_groups,),
            in_specs=[
                pl.BlockSpec((quad_pairs, 8, length), lambda g, base=base: (base + g, 0, 0)),
                quad_spec,
                quad_spec,
                full((length, STATE)),
                full((length, STATE)),
                full((1, length)),
                full((length, 1)),
            ]
            + ([full((length, length)), pl.BlockSpec(memory_space=pl.ANY)] if part else []),
            out_specs=[
                quad_spec,
                pl.BlockSpec((1, 2 * quad_pairs, length), lambda g: (g, 0, 0)),
                full((length, length)),
            ],
            out_shape=[
                jax.ShapeDtypeStruct((length, width), f32),
                jax.ShapeDtypeStruct((quad_groups, 2 * quad_pairs, length), f32),
                jax.ShapeDtypeStruct((length, length), f32),
            ],
            scratch_shapes=[pltpu.VMEM((length, length), f32)],
            input_output_aliases={8: 0} if part else {},
            compiler_params=limit,
            cost_estimate=pl.CostEstimate(
                flops=50_000_000_000 // parts, bytes_accessed=20_000_000 // parts, transcendentals=0
            ),
            name="quad",
        )(aux, x_rows, dy_rows, b_half, c_half, labr, labc, *([mixed, r_local] if part else []))
        a_parts.append(a_part.reshape(-1, length))
    a_sum = jnp.concatenate(a_parts, axis=0)
    keep = (positions[:, None] <= positions[None, :]) & (labc == labr)
    mixed = jnp.where(keep, mixed, 0.0).astype(bf16)
    local_b = jnp.dot(mixed, c_half, preferred_element_type=f32)
    local_c = mm(mixed, b_half, 0, 0) + state_term

    grad_x, u_sum, bgrad, vw = pl.pallas_call(
        functools.partial(leave_kernel, wide_pairs),
        grid=(groups,),
        in_specs=[aux_spec, col_spec, col_spec, full((length, STATE)), row_spec, row_spec],
        out_specs=[
            col_spec,
            full((length, 128)),
            full((length, STATE)),
            pl.BlockSpec((wide_pairs, 8, STATE), lambda g: (g, 0, 0)),
        ],
        out_shape=[
            jax.ShapeDtypeStruct((length, width), bf16),
            jax.ShapeDtypeStruct((length, 128), f32),
            jax.ShapeDtypeStruct((length, STATE), f32),
            jax.ShapeDtypeStruct((pair_count, 8, STATE), f32),
        ],
        compiler_params=limit,
        name="leave",
    )(aux, x_rows, r_local, b_half, carry, states)
    v_term = ends * jnp.sum(vw[:, 0:2], axis=2).reshape(head_count)
    w_sum = jnp.sum(vw[:, 2].reshape(head_count, HEAD_DIM), axis=1)
    u_rows = u_sum[:, :head_count].T
    cum_grad = a_sum + enter_out[:, :head_count].T - u_rows
    tail_sum = mm_high(cum_grad, upto, high) + (v_term + w_sum)[:, None]
    step_grad = u_rows / steps + decay_rate[:, None] * tail_sum
    dt_grad = (step_grad * jax.nn.sigmoid(raw_steps)).astype(bf16)

    tp = lax.axis_size("tp")
    maps = jnp.concatenate([local_b + bgrad, local_c], axis=1).astype(bf16)
    maps = lax.all_to_all(maps.reshape(tp, length // tp, 2 * STATE), "tp", 0, 0)
    grad_maps = jnp.sum(maps.astype(f32), axis=0)

    gathered = lax.all_gather(dt_grad, "tp", axis=0, tiled=True)
    replicas = lax.axis_size("dp") * count
    product = jnp.dot(gathered, layer_in[0], preferred_element_type=f32).astype(bf16)
    product = product.reshape(replicas, gathered.shape[0] // replicas, width)
    summed = jnp.sum(lax.all_to_all(product, ("dp", "ctx"), 0, 0).astype(f32), axis=0)
    squares = jnp.sum(summed * summed, axis=1)
    own_norm = jnp.sqrt(lax.psum(squares, "tp") + epsilon)
    target = jnp.sum(lax.all_gather(own_norm, ("dp", "ctx"))) / gathered.shape[0]
    grad_dt_proj = summed * jnp.minimum(1.0, target / own_norm)[:, None]
    return (grad_x[None], grad_maps[None], grad_dt_proj)


def mm_high(a, b, precision):
    return lax.dot_general(a, b, (((1,), (1,)), ((), ())), precision=precision, preferred_element_type=f32)


def solution(mesh):
    in_specs = (
        P("dp", "ctx", "tp"),
        P("dp", "ctx", "tp"),
        P("dp", "ctx", None),
        P("dp", "tp", "ctx"),
        P("tp"),
        P("dp", "ctx", "tp", None, None),
        P("dp", "ctx", "tp"),
        P("dp", None),
    )
    out_specs = (P("dp", "ctx", "tp"), P("dp", ("ctx", "tp"), None), P(("dp", "ctx"), "tp"))
    return jax.shard_map(shards, mesh=mesh, in_specs=in_specs, out_specs=out_specs, check_vma=False)
```

time: 456 us -> 215 us (0.47)
  matrix products: 174 us -> 7.59 us
  other arithmetic: 83.8 us -> 15.1 us
  Pallas kernels: 0 us -> 60.4 us
  local copies, waits for them, and re-layouts: 65.8 us -> 36.9 us
  blocking collectives: 62.8 us -> 41.8 us
  starting transfers between devices: 0.35 us -> 16.9 us
  waiting for transfers between devices: 47.4 us -> 31.9 us
  between operations: 18 us -> 3.03 us
    dot_general x41 -> x5, matrix products: 174 us -> 7.59 us  [the longest x1 3.99 us: shards(): jnp.dot(gathered, layer_in[0], preferred_element_type=f32).astype(bf16)]
    pallas_call x0 -> x6, Pallas kernels: none -> 60.4 us  [the longest x4 31 us: shards(): pl.pallas_call(functools.partial(quad_kernel, quad_pairs), grid=(quad_gro...]
    reduce_scatter x3 -> x0, waiting for transfers between devices: 47.3 us -> none  [the longest x1 47.3 us: shards(): lax.psum_scatter(jnp.dot(gathered, tokens_in, preferred_element_type=jnp....]
    psum x1 -> x0, blocking collectives: 35.6 us -> none  [shards(): target = lax.psum(jnp.sum(own_norm), ('dp', 'ctx')) / gathered.shape[0]]
    add x18 -> x1, other arithmetic: 28.2 us -> 0.7 us  [shards(): tail_sum = mm_high(cum_grad, upto, high) + (v_term + w_sum)[:, None]]
    all_to_all x0 -> x2, waiting for transfers between devices: none -> 26.1 us  [the longest x1 22.4 us: shards(): lax.all_to_all(product, ('dp', 'ctx'), 0, 0).astype(f32)]
    unnamed x1, blocking collectives: 19.5 us -> 34.1 us
    rev x4 -> x0, local copies, waits for them, and re-layouts: 13.9 us -> none  [the longest x2 11.8 us: prefix(): pieces = jax.tree.map(lambda part: part[::-1], pieces)]
  transfers between devices with their start and end apart: 4 -> 7, of which waited for: 1 -> 3; matrix products, arithmetic and copies ran while one was open for 65% -> 3% of each run, Pallas kernels for 0% -> 15%
where the time goes in v1:
time: 215 us; the launch traced here: 214 us
  Pallas kernels  60.4 us (28%)
  blocking collectives  41.8 us (19%)
  local copies, waits for them, and re-layouts  36.9 us (17%)
  waiting for transfers between devices  31.9 us (15%)
  starting transfers between devices  16.9 us (8%)
  other arithmetic  15.1 us (7%)
  matrix products  7.59 us (4%)
  between operations  3.03 us (1%)
    unnamed x1, blocking collectives  34.1 us
    pallas_call x4, Pallas kernels, shards(): pl.pallas_call(functools.partial(quad_kernel, quad_pairs), grid=(quad_gro...  31 us
    all_to_all x1, waiting for transfers between devices, shards(): lax.all_to_all(product, ('dp', 'ctx'), 0, 0).astype(f32)  22.4 us
    unnamed x51, local copies, waits for them, and re-layouts  21.6 us
    pallas_call x1, Pallas kernels, shards(): pl.pallas_call(functools.partial(enter_kernel, wide_pairs), grid=(groups,...  16.4 us
    pallas_call x1, Pallas kernels, shards(): pl.pallas_call(functools.partial(leave_kernel, wide_pairs), grid=(groups,...  12.9 us
    all_to_all x1, starting transfers between devices, shards(): lax.all_to_all(product, ('dp', 'ctx'), 0, 0).astype(f32)  8.64 us
    ppermute x2, waiting for transfers between devices, shift(): return jax.tree.map(lambda part: lax.ppermute(part, 'ctx', moves), value)  5.76 us
  transfers between devices with their start and end apart: 7, of which 3 were waited for; matrix products, arithmetic and copies ran while one was open for 3% of the time, Pallas kernels for 15%

profile of v1, /device:TPU:1, one launch (start us, length us, event | category | flops | bytes accessed | tf_op | source)
XLA Modules:
  0.0 213.6 jit_solution(10903771595896601599)
XLA Ops:
  0.6 1.0 copy.104
  1.7 0.7 exponential_negate_fusion
  2.4 0.6 fusion.12
  3.3 1.0 reduce-window.8
  4.4 0.6 slice.28
  5.0 0.6 fusion.39
  6.2 0.7 compare_convert_fusion.2
  6.9 1.0 multiply_subtract_fusion
  8.1 1.1 copy.112
  9.6 0.2 maximum_bitcast_fusion
  9.9 0.4 reshape.99.aux_ref
  10.3 1.0 slice_bitcast_fusion
  11.3 2.2 %copy-done.2 = bf16[1,512,4096]{2,1,0:T(8,128)(2,1)S(1)} copy-done((bf16[1,512,4096]{2,1,0:T(8,128)(2,1)S(1)}, bf16[1,512,4096]{2,1,0:T(8,128)(2,1)}, u32[]{:S(2)}) %copy-start.2) | copy-done | bytes 4194328
  13.5 16.4 %enter.1 = (bf16[4096,128]{1,0:T(8,128)(2,1)S(1)}, f32[512,128]{1,0:T(8,128)S(1)}, f32[512,128]{1,0:T(8,128)S(1)}) custom-call(f32[32,8,512]{2,1,0:T(8,128)S(1)} %reshape.99.aux_ref, bf16[512,4096]{1,0:T(8,128)(2,1)S(1)} %bitcast.109, bf16[512,128]{1,0:T(8,128)(2,1)S(1)} %get-tuple-element.45.c_ref, f32[4096,128]{1,0:T(8,128)S(1)} %bitcast.107), custom_call_target="tpu_custom_call" | custom-call | tf_op jit(solution)/shard_map/enter/pallas_call | solution.py:202
  30.0 1.0 copy-done.8
  30.9 2.4 %reshape.101 = bf16[2,32,8192]{2,1,0:T(8,128)(2,1)} reshape(bf16[4096,128]{1,0:T(8,128)(2,1)} %copy-done.8) | data formatting | bytes 2097152 | tf_op jit(solution)/shard_map/reshape | solution.py:223
  33.4 1.9 dynamic-slice_bitcast_fusion
  35.2 2.0 collective-permute-start
  37.3 0.7 slice_reduce_fusion.3
  38.2 2.2 %copy-done.3 = bf16[1,512,4096]{2,1,0:T(8,128)(2,1)S(1)} copy-done((bf16[1,512,4096]{2,1,0:T(8,128)(2,1)S(1)}, bf16[1,512,4096]{2,1,0:T(8,128)(2,1)}, u32[]{:S(2)}) %copy-start.3) | copy-done | bytes 4194328
  40.4 2.2 %copy-done.5 = bf16[1,512,4096]{2,1,0:T(8,128)(2,1)S(1)} copy-done((bf16[1,512,4096]{2,1,0:T(8,128)(2,1)S(1)}, bf16[1,512,4096]{2,1,0:T(8,128)(2,1)}, u32[]{:S(2)}) %copy-start.5) | copy-done | bytes 4194328
  42.6 7.7 %quad.4 = (f32[512,4096]{1,0:T(8,128)}, f32[4,4,512]{2,1,0:T(4,128)S(1)}, f32[512,512]{1,0:T(8,128)S(1)}) custom-call(f32[32,8,512]{2,1,0:T(8,128)S(1)} %reshape.99.aux_ref, bf16[512,4096]{1,0:T(8,128)(2,1)S(1)} %bitcast.114, bf16[512,4096]{1,0:T(8,128)(2,1)S(1)} %bitcast.110, bf16[512,128]{1,0:T(8,128)(2,1)S(1)} %get-tuple-element.46.b_ref, ...), custom_call_target="tpu_custom_call" | custom-call | flops 12499999744 | bytes 5000000 | tf_op jit(solution)/shard_map/quad/pallas_call | solution.py:256
  50.3 1.0 copy-done.16
  51.3 1.4 fusion.9
  52.8 1.3 collective-permute-start.2
  54.1 2.2 %copy-done.4 = bf16[1,512,4096]{2,1,0:T(8,128)(2,1)S(1)} copy-done((bf16[1,512,4096]{2,1,0:T(8,128)(2,1)S(1)}, bf16[1,512,4096]{2,1,0:T(8,128)(2,1)}, u32[]{:S(2)}) %copy-start.4) | copy-done | bytes 4194328
  56.2 2.2 %copy-done.6 = bf16[1,512,4096]{2,1,0:T(8,128)(2,1)S(1)} copy-done((bf16[1,512,4096]{2,1,0:T(8,128)(2,1)S(1)}, bf16[1,512,4096]{2,1,0:T(8,128)(2,1)}, u32[]{:S(2)}) %copy-start.6) | copy-done | bytes 4194328
  58.4 1.2 copy-done.17
  59.7 7.7 %quad.5 = (f32[512,4096]{1,0:T(8,128)}, f32[4,4,512]{2,1,0:T(4,128)S(1)}, f32[512,512]{1,0:T(8,128)S(1)}) custom-call(f32[32,8,512]{2,1,0:T(8,128)S(1)} %reshape.99.aux_ref, bf16[512,4096]{1,0:T(8,128)(2,1)S(1)} %bitcast.115, bf16[512,4096]{1,0:T(8,128)(2,1)S(1)} %bitcast.111, ...), custom_call_target="tpu_custom_call", output_to_operand_aliasing={{0}: (8, {})} | custom-call | flops 12499999744 | bytes 5000000 | tf_op jit(solution)/shard_map/quad/pallas_call | solution.py:256
  67.4 0.2 add_convert_fusion
  67.6 1.5 collective-permute-start.3
  69.1 7.8 %quad.6 = (f32[512,4096]{1,0:T(8,128)}, f32[4,4,512]{2,1,0:T(4,128)S(1)}, f32[512,512]{1,0:T(8,128)S(1)}) custom-call(f32[32,8,512]{2,1,0:T(8,128)S(1)} %reshape.99.aux_ref, bf16[512,4096]{1,0:T(8,128)(2,1)S(1)} %bitcast.116, bf16[512,4096]{1,0:T(8,128)(2,1)S(1)} %bitcast.112, ...), custom_call_target="tpu_custom_call", output_to_operand_aliasing={{0}: (8, {})} | custom-call | flops 12499999744 | bytes 5000000 | tf_op jit(solution)/shard_map/quad/pallas_call | solution.py:256
  76.9 5.8 %collective-permute-done.3 = bf16[32,8192]{1,0:T(8,128)(2,1)S(1)} collective-permute-done((bf16[32,8192]{1,0:T(8,128)(2,1)S(1)}, bf16[32,8192]{1,0:T(8,128)(2,1)S(1)}, u32[]{:S(2)}, u32[]{:S(2)}) %collective-permute-start.3) | collective-permute-done | bytes 524320 | tf_op jit(solution)/shard_map/ppermute | solution.py:167
  82.7 2.4 %fusion.15 = (bf16[1,32,8192]{2,1,0:T(8,128)(2,1)}, bf16[32,8192]{1,0:T(8,128)(2,1)}) fusion(bf16[32,8192]{1,0:T(8,128)(2,1)S(1)} %collective-permute-done.3, f32[32]{0:T(128)S(1)} %get-tuple-element.51, pred[]{:T(512)S(6)} %eq.48, bf16[32,8192]{1,0:T(8,128)(2,1)} %collective-permute-done, bf16[2,32,8192]{2,1,0:T(8,128)(2,1)S(1)} %copy-done.18, s32[]{:T(128)S(6)} %select_n.79), kind=kLoop, calls=%fused_computation.27 | loop fusion | flops 2097152 | bytes 2621573 | tf_op jit(solution)/shard_map/stack | solution.py:244
  85.1 7.8 %quad.7 = (f32[512,4096]{1,0:T(8,128)}, f32[4,4,512]{2,1,0:T(4,128)S(1)}, f32[512,512]{1,0:T(8,128)S(1)}) custom-call(f32[32,8,512]{2,1,0:T(8,128)S(1)} %reshape.99.aux_ref, bf16[512,4096]{1,0:T(8,128)(2,1)S(1)} %bitcast.117, bf16[512,4096]{1,0:T(8,128)(2,1)S(1)} %bitcast.113, ...), custom_call_target="tpu_custom_call", output_to_operand_aliasing={{0}: (8, {})} | custom-call | flops 12499999744 | bytes 5000000 | tf_op jit(solution)/shard_map/quad/pallas_call | solution.py:256
  92.9 1.1 copy-done.14
  93.9 0.8 copy.123
  94.8 0.8 copy.122
  95.6 0.8 copy.121
  96.5 0.8 copy.120
  97.3 2.7 %maximum_select_fusion = bf16[2,32,8192]{2,1,0:T(8,128)(2,1)} fusion(bf16[1,32,8192]{2,1,0:T(8,128)(2,1)} %bitcast.17, bf16[1,32,8192]{2,1,0:T(8,128)(2,1)} %get-tuple-element.41, pred[]{:T(512)S(6)} %eq.48), kind=kLoop, calls=%fused_computation.18 | loop fusion | flops 1572864 | bytes 2097153 | tf_op jit(solution)/shard_map/jit(_where)/select_n | solution.py:244
  100.0 2.3 %select_n.88.carry_ref = bf16[4096,128]{1,0:T(8,128)(2,1)} reshape(bf16[2,32,8192]{2,1,0:T(8,128)(2,1)} %maximum_select_fusion) | data formatting | bytes 2097152 | tf_op jit(solution)/shard_map/jit(_where)/select_n | solution.py:244
  102.3 1.2 copy-done.1
  103.5 2.2 %copy-done.7 = bf16[1,512,4096]{2,1,0:T(8,128)(2,1)S(1)} copy-done((bf16[1,512,4096]{2,1,0:T(8,128)(2,1)S(1)}, bf16[1,512,4096]{2,1,0:T(8,128)(2,1)}, u32[]{:S(2)}) %copy-start.7) | copy-done | bytes 4194328
  105.7 12.9 %leave.1 = (bf16[512,4096]{1,0:T(8,128)(2,1)}, f32[512,128]{1,0:T(8,128)S(1)}, f32[512,128]{1,0:T(8,128)S(1)}, f32[32,8,128]{2,1,0:T(8,128)S(1)}) custom-call(f32[32,8,512]{2,1,0:T(8,128)S(1)} %reshape.99.aux_ref, bf16[512,4096]{1,0:T(8,128)(2,1)S(1)} %bitcast.118, f32[512,4096]{1,0:T(8,128)} %get-tuple-element.28.r_ref, ...), custom_call_target="tpu_custom_call" | custom-call | tf_op jit(solution)/shard_map/leave/pallas_call | solution.py:294
  118.7 0.7 copy-done.11
  119.4 0.7 copy-done.13
  120.5 0.7 fusion.40
  121.2 2.3 %fusion.7 = bf16[64,512]{0,1:T(8,128)(2,1)S(1)} fusion(f32[16,512]{0,1:T(8,128)} %copy.123, f32[16,512]{0,1:T(8,128)} %copy.122, f32[16,512]{0,1:T(8,128)} %copy.121, f32[16,512]{0,1:T(8,128)} %copy.120, f32[1,64,512]{1,2,0:T(8,128)S(1)} %copy-done.21, f32[512,128]{1,0:T(8,128)S(1)} %copy-done.10, f32[512,128]{1,0:T(8,128)} %copy-done.13, ...), kind=kOutput, calls=%fused_computation.14 | convolution fusion | flops 202244096 | bytes 2032128 | tf_op jit(solution)/shard_map/dot_general | solution.py:339
  123.6 3.9 %all_gather.9 = bf16[128,512]{1,0:T(8,128)(2,1)S(1)} all-gather(bf16[64,512]{1,0:T(8,128)(2,1)S(1)} %copy.125), channel_id=1, replica_groups=mesh['dp'=2,'ctx'=8,'tp'=2] {'tp'}, dimensions={0}, use_global_device_ids=true | all-gather | bytes 196608 | tf_op jit(solution)/shard_map/all_gather | solution.py:326
  127.5 4.0 %fusion = bf16[16,8,4096]{2,1,0:T(8,128)(2,1)} fusion(bf16[128,512]{1,0:T(8,128)(2,1)S(1)} %all_gather.9, bf16[1,512,4096]{2,1,0:T(8,128)(2,1)} %param.14), kind=kOutput, calls=%fused_computation.1 | convolution fusion | flops 537395200 | bytes 5373952 | tf_op jit(solution)/shard_map/dot_general | solution.py:328
  131.5 8.6 %all-to-all-start.1 = ((bf16[16,8,4096]{2,1,0:T(8,128)(2,1)}), bf16[16,8,4096]{2,1,0:T(8,128)(2,1)S(1)}, u32[]{:S(2)}, u32[]{:S(2)}) async-start(bf16[16,8,4096]{2,1,0:T(8,128)(2,1)} %fusion), calls=%async_computation.1 | async-start | bytes 2097152 | tf_op jit(solution)/shard_map/all_to_all | solution.py:330
  140.2 0.6 dynamic-slice
  141.4 0.4 fusion.6
  141.9 0.4 fusion.5
  142.2 0.7 pad_maximum_fusion
  143.0 22.4 %all-to-all-done.1 = bf16[16,8,4096]{2,1,0:T(8,128)(2,1)S(1)} async-done(((bf16[16,8,4096]{2,1,0:T(8,128)(2,1)}), bf16[16,8,4096]{2,1,0:T(8,128)(2,1)S(1)}, u32[]{:S(2)}, u32[]{:S(2)}) %all-to-all-start.1) | async-done | bytes 1048608 | tf_op jit(solution)/shard_map/all_to_all | solution.py:330
  165.4 3.4 %all-to-all-start = ((bf16[2,256,256]{2,1,0:T(8,128)(2,1)}), bf16[2,256,256]{2,1,0:T(8,128)(2,1)S(1)}, u32[]{:S(2)}, u32[]{:S(2)}) async-start(bf16[2,256,256]{2,1,0:T(8,128)(2,1)} %pad_maximum_fusion), calls=%async_computation | async-start | bytes 524288 | tf_op jit(solution)/shard_map/all_to_all | solution.py:323
  169.1 3.7 %all-to-all-done = bf16[2,256,256]{2,1,0:T(8,128)(2,1)S(1)} async-done(((bf16[2,256,256]{2,1,0:T(8,128)(2,1)}), bf16[2,256,256]{2,1,0:T(8,128)(2,1)S(1)}, u32[]{:S(2)}, u32[]{:S(2)}) %all-to-all-start) | async-done | bytes 262176 | tf_op jit(solution)/shard_map/all_to_all | solution.py:323
  172.9 0.7 convert_reduce_fusion.1
  173.6 3.8 %psum.7 = f32[8]{0:T(128)S(1)} all-reduce(f32[8]{0:T(128)S(1)} %multiply_reduce_fusion), channel_id=1, replica_groups=mesh['dp'=2,'ctx'=8,'tp'=2] {'tp'}, use_global_device_ids=true, to_apply=%region_8.9 | all-reduce | flops 8 | bytes 64 | tf_op jit(solution)/shard_map/psum | solution.py:332
  177.5 34.1 %all-reduce = f32[128]{0:T(128)S(1)} all-reduce(f32[128]{0:T(128)S(1)} %fusion.41), channel_id=2, replica_groups=mesh['dp'=2,'ctx'=8,'tp'=2] {'dp','ctx'}, use_global_device_ids=true, to_apply=%add | all-reduce | flops 128 | bytes 1024
  211.6 0.6 reduce_sum.85
  212.8 0.7 broadcast_multiply_fusion.1
  (72 shorter events, 2.4 us)
Async XLA Ops:
  1.7 8.2 %copy-start.20 = (f32[1,64,512]{1,2,0:T(8,128)}, f32[1,64,512]{1,2,0:T(8,128)S(1)}, u32[]{:S(2)}) copy-start(f32[1,64,512]{1,2,0:T(8,128)S(1)} %copy.104) | copy-start | bytes 393220
  2.9 8.4 %copy-start = (f32[1,1,64,64,128]{4,3,2,1,0:T(8,128)S(1)}, f32[1,1,64,64,128]{4,3,2,1,0:T(8,128)}, u32[]{:S(2)}) copy-start(f32[1,1,64,64,128]{4,3,2,1,0:T(8,128)} %param.13) | copy-start | bytes 6291460
  7.9 3.4 %copy-start.19 = (f32[64,512]{0,1:T(8,128)}, f32[64,512]{0,1:T(8,128)S(1)}, u32[]{:S(2)}) copy-start(f32[64,512]{0,1:T(8,128)S(1)} %get-tuple-element.48) | copy-start | bytes 393220
  11.3 2.2 %copy-start.2 = (bf16[1,512,4096]{2,1,0:T(8,128)(2,1)S(1)}, bf16[1,512,4096]{2,1,0:T(8,128)(2,1)}, u32[]{:S(2)}) copy-start(bf16[1,512,4096]{2,1,0:T(8,128)(2,1)} %param.9) | copy-start | bytes 12582916
  29.9 1.0 copy-start.8
  30.9 7.2 %copy-start.9 = (f32[512,128]{1,0:T(8,128)}, f32[512,128]{1,0:T(8,128)S(1)}, u32[]{:S(2)}) copy-start(f32[512,128]{1,0:T(8,128)S(1)} %get-tuple-element.39) | copy-start | bytes 786436
  35.2 16.1 %collective-permute-start = (bf16[32,8192]{1,0:T(8,128)(2,1)}, bf16[32,8192]{1,0:T(8,128)(2,1)}, u32[]{:S(2)}, u32[]{:S(2)}) collective-permute-start(bf16[32,8192]{1,0:T(8,128)(2,1)} %dynamic-slice_bitcast_fusion), channel_id=1, source_target_pairs={{0,2},{2,0},{4,6},{6,4},{8,10},{10,8},{12,14},{14,12},{1,3},{3,1},... | collective-permute-start | bytes 1572872 | tf_op jit(solution)/shard_map/ppermute | solution.py:226
  38.1 13.2 %collective-permute-start.1 = (f32[32]{0:T(128)S(1)}, f32[32]{0:T(128)S(1)}, u32[]{:S(2)}, u32[]{:S(2)}) collective-permute-start(f32[32]{0:T(128)S(1)} %fusion.37), channel_id=1, source_target_pairs={{0,2},{2,0},{4,6},{6,4},{8,10},{10,8},{12,14},{14,12},{1,3},{3,1},... | collective-permute-start | bytes 392 | tf_op jit(solution)/shard_map/ppermute | solution.py:227
  38.2 2.2 %copy-start.3 = (bf16[1,512,4096]{2,1,0:T(8,128)(2,1)S(1)}, bf16[1,512,4096]{2,1,0:T(8,128)(2,1)}, u32[]{:S(2)}) copy-start(bf16[1,512,4096]{2,1,0:T(8,128)(2,1)} %param.9) | copy-start | bytes 12582916
  40.4 2.2 %copy-start.5 = (bf16[1,512,4096]{2,1,0:T(8,128)(2,1)S(1)}, bf16[1,512,4096]{2,1,0:T(8,128)(2,1)}, u32[]{:S(2)}) copy-start(bf16[1,512,4096]{2,1,0:T(8,128)(2,1)} %param.8) | copy-start | bytes 12582916
  50.3 1.0 copy-start.16
  52.8 14.6 %collective-permute-start.2 = (bf16[32,8192]{1,0:T(8,128)(2,1)S(1)}, bf16[32,8192]{1,0:T(8,128)(2,1)S(1)}, u32[]{:S(2)}, u32[]{:S(2)}) collective-permute-start(bf16[32,8192]{1,0:T(8,128)(2,1)S(1)} %fusion.9), channel_id=1, source_target_pairs={{4,0},{6,2},{8,4},{10,6},{12,8},{14,10},{5,1},{7,3},{9,5},{11,7},{... | collective-permute-start | bytes 1572872 | tf_op jit(solution)/shard_map/ppermute | solution.py:167
  54.1 2.2 %copy-start.4 = (bf16[1,512,4096]{2,1,0:T(8,128)(2,1)S(1)}, bf16[1,512,4096]{2,1,0:T(8,128)(2,1)}, u32[]{:S(2)}) copy-start(bf16[1,512,4096]{2,1,0:T(8,128)(2,1)} %param.9) | copy-start | bytes 12582916
  56.2 2.2 %copy-start.6 = (bf16[1,512,4096]{2,1,0:T(8,128)(2,1)S(1)}, bf16[1,512,4096]{2,1,0:T(8,128)(2,1)}, u32[]{:S(2)}) copy-start(bf16[1,512,4096]{2,1,0:T(8,128)(2,1)} %param.8) | copy-start | bytes 12582916
  58.4 1.2 copy-start.17
  67.6 15.1 %collective-permute-start.3 = (bf16[32,8192]{1,0:T(8,128)(2,1)S(1)}, bf16[32,8192]{1,0:T(8,128)(2,1)S(1)}, u32[]{:S(2)}, u32[]{:S(2)}) collective-permute-start(bf16[32,8192]{1,0:T(8,128)(2,1)S(1)} %add_convert_fusion), channel_id=1, source_target_pairs={{4,0},{6,2},{8,4},{10,6},{12,8},{14,10},{5,1},{7,3},{9,5},{11,7},{... | collective-permute-start | bytes 1572872 | tf_op jit(solution)/shard_map/ppermute | solution.py:167
  69.1 13.6 %copy-start.18 = (bf16[2,32,8192]{2,1,0:T(8,128)(2,1)S(1)}, bf16[2,32,8192]{2,1,0:T(8,128)(2,1)}, u32[]{:S(2)}) copy-start(bf16[2,32,8192]{2,1,0:T(8,128)(2,1)} %reshape.101) | copy-start | bytes 3145732
  85.0 12.3 %collective-permute-start.4 = (bf16[32,8192]{1,0:T(8,128)(2,1)}, bf16[32,8192]{1,0:T(8,128)(2,1)}, u32[]{:S(2)}, u32[]{:S(2)}) collective-permute-start(bf16[32,8192]{1,0:T(8,128)(2,1)} %get-tuple-element.42), channel_id=1, source_target_pairs={{0,2},{2,0},{4,6},{6,4},{8,10},{10,8},{12,14},{14,12},{1,3},{3,1},... | collective-permute-start | bytes 1572872 | tf_op jit(solution)/shard_map/ppermute | solution.py:242
  92.9 1.1 copy-start.14
  102.3 1.2 copy-start.1
  103.5 2.2 %copy-start.7 = (bf16[1,512,4096]{2,1,0:T(8,128)(2,1)S(1)}, bf16[1,512,4096]{2,1,0:T(8,128)(2,1)}, u32[]{:S(2)}) copy-start(bf16[1,512,4096]{2,1,0:T(8,128)(2,1)} %param.8) | copy-start | bytes 12582916
  105.7 15.5 %copy-start.10 = (f32[512,128]{1,0:T(8,128)S(1)}, f32[512,128]{1,0:T(8,128)}, u32[]{:S(2)}) copy-start(f32[512,128]{1,0:T(8,128)} %copy-done.9) | copy-start | bytes 786436
  105.7 15.5 %copy-start.21 = (f32[1,64,512]{1,2,0:T(8,128)S(1)}, f32[1,64,512]{1,2,0:T(8,128)}, u32[]{:S(2)}) copy-start(f32[1,64,512]{1,2,0:T(8,128)} %copy-done.20) | copy-start | bytes 393220
  118.7 0.7 copy-start.11
  119.4 0.7 copy-start.13
  123.5 16.7 %copy-start.23 = (u32[32]{0:T(128)S(1)}, u32[32]{0:T(128)}, u32[]{:S(2)}) copy-start(u32[32]{0:T(128)} %constant.66) | copy-start | bytes 388
  123.5 17.9 %copy-start.15 = (f32[512,512]{1,0:T(8,128)S(1)}, f32[512,512]{1,0:T(8,128)}, u32[]{:S(2)}) copy-start(f32[512,512]{1,0:T(8,128)} %copy-done.14) | copy-start | bytes 3145732
  123.5 17.9 %copy-start.22 = (bf16[1,512,256]{2,1,0:T(8,128)(2,1)S(1)}, bf16[1,512,256]{2,1,0:T(8,128)(2,1)}, u32[]{:S(2)}) copy-start(bf16[1,512,256]{2,1,0:T(8,128)(2,1)} %param.10) | copy-start | bytes 786436
  127.5 14.3 %copy-start.12 = (f32[512,128]{1,0:T(8,128)S(1)}, f32[512,128]{1,0:T(8,128)}, u32[]{:S(2)}) copy-start(f32[512,128]{1,0:T(8,128)} %copy-done.11) | copy-start | bytes 786436
  131.5 33.9 %all-to-all-start.1 = ((bf16[16,8,4096]{2,1,0:T(8,128)(2,1)}), bf16[16,8,4096]{2,1,0:T(8,128)(2,1)S(1)}, u32[]{:S(2)}, u32[]{:S(2)}) async-start(bf16[16,8,4096]{2,1,0:T(8,128)(2,1)} %fusion), calls=%async_computation.1 | async-start | bytes 2097152 | tf_op jit(solution)/shard_map/all_to_all | solution.py:330
  165.4 7.5 %all-to-all-start = ((bf16[2,256,256]{2,1,0:T(8,128)(2,1)}), bf16[2,256,256]{2,1,0:T(8,128)(2,1)S(1)}, u32[]{:S(2)}, u32[]{:S(2)}) async-start(bf16[2,256,256]{2,1,0:T(8,128)(2,1)} %pad_maximum_fusion), calls=%async_computation | async-start | bytes 524288 | tf_op jit(solution)/shard_map/all_to_all | solution.py:323

commit v2 on v1

--- a/solution.py
+++ b/solution.py
@@ -21,18 +21,23 @@
     return lax.dot_general(a, b, (((ca,), (cb,)), ((), ())), preferred_element_type=f32)
 
 
-def spread(cols, first, second, rows):
-    lane = lax.broadcasted_iota(jnp.int32, (rows, PAIR), 1)
-    return jnp.where(lane < HEAD_DIM, cols[:, first : first + 1], cols[:, second : second + 1])
-
-
-def head_sums(value, pair):
+def spread(rows):
+    heads = rows.shape[0]
+    high = rows.astype(bf16).astype(f32)
+    both = jnp.concatenate([high, rows - high], axis=0).astype(bf16)
+    row = lax.broadcasted_iota(jnp.int32, (2 * heads, heads * HEAD_DIM), 0) % heads
+    head = lax.broadcasted_iota(jnp.int32, (2 * heads, heads * HEAD_DIM), 1) // HEAD_DIM
+    return mm(both, jnp.where(row == head, 1.0, 0.0).astype(bf16), 0, 0)
+
+
+def head_sums(value, first):
+    width = value.shape[1]
     high = value.astype(bf16)
     low = (value - high.astype(f32)).astype(bf16)
-    row = lax.broadcasted_iota(jnp.int32, (2 * PAIR, 128), 0) % PAIR
-    col = lax.broadcasted_iota(jnp.int32, (2 * PAIR, 128), 1)
-    chosen = col == 2 * pair + jnp.where(row >= HEAD_DIM, 1, 0)
-    return mm(jnp.concatenate([high, low], axis=1), jnp.where(chosen, 1.0, 0.0).astype(bf16), 1, 0)
+    row = lax.broadcasted_iota(jnp.int32, (2 * width, 128), 0) % width
+    col = lax.broadcasted_iota(jnp.int32, (2 * width, 128), 1)
+    chosen = jnp.where(col == first + row // HEAD_DIM, 1.0, 0.0).astype(bf16)
+    return mm(jnp.concatenate([high, low], axis=1), chosen, 1, 0)
 
 
 def enter_kernel(pairs, aux_ref, dy_ref, c_ref, s_ref, local_ref, sterm_ref, eo_ref):
@@ -43,17 +48,14 @@
         sterm_ref[...] = jnp.zeros_like(sterm_ref)
         eo_ref[...] = jnp.zeros_like(eo_ref)
 
-    rows = dy_ref.shape[0]
     c_rows = c_ref[...]
-    for p in range(pairs):
-        at = slice(p * PAIR, (p + 1) * PAIR)
-        cols = aux_ref[p].T
-        wide = dy_ref[:, at].astype(f32) * spread(cols, 6, 7, rows)
-        scaled = wide.astype(bf16)
-        local_ref[at, :] = mm(scaled, c_rows, 0, 0).astype(bf16)
-        state = s_ref[at, :].astype(bf16)
-        sterm_ref[...] += mm(scaled, state, 1, 0)
-        eo_ref[...] += head_sums(wide * mm(c_rows, state, 1, 1), step * pairs + p)
+    enter = jnp.concatenate([aux_ref[p][6:8] for p in range(pairs)], axis=0)
+    wide = dy_ref[...].astype(f32) * spread(enter)
+    scaled = wide.astype(bf16)
+    local_ref[...] = mm(c_rows, scaled, 0, 0).T.astype(bf16)
+    state = s_ref[...].astype(bf16)
+    sterm_ref[...] += mm(scaled, state, 1, 0)
+    eo_ref[...] += head_sums(wide * mm(c_rows, state, 1, 1), step * 2 * pairs)
 
 
 def quad_kernel(
@@ -128,23 +130,110 @@
         u_ref[...] = jnp.zeros_like(u_ref)
         bgrad_ref[...] = jnp.zeros_like(bgrad_ref)
 
-    rows = x_ref.shape[0]
+    weight = spread(jnp.concatenate([aux_ref[p][4:6] for p in range(pairs)], axis=0))
+    carry = carry_ref[...]
+    x = x_ref[...].astype(f32)
+    after = weight * mm(b_ref[...], carry, 1, 1)
+    grad = r_ref[...] + after
+    gx_ref[...] = grad.astype(bf16)
+    u_ref[...] += head_sums(x * grad, step * 2 * pairs)
+    bgrad_ref[...] += mm((weight * x).astype(bf16), carry, 1, 0)
+    w_sums = jnp.sum(x * after, axis=0, keepdims=True)
+    both = carry.astype(f32) * s_ref[...]
     for p in range(pairs):
-        at = slice(p * PAIR, (p + 1) * PAIR)
-        cols = aux_ref[p].T
-        weight = spread(cols, 4, 5, rows)
-        carry = carry_ref[at, :]
-        x = x_ref[:, at].astype(f32)
-        after = weight * mm(b_ref[...], carry, 1, 1)
-        grad = r_ref[:, at] + after
-        gx_ref[:, at] = grad.astype(bf16)
-        u_ref[...] += head_sums(x * grad, step * pairs + p)
-        bgrad_ref[...] += mm((weight * x).astype(bf16), carry, 1, 0)
-        both = carry.astype(f32) * s_ref[at, :]
-        vw_ref[p, 0:1, :] = jnp.sum(both[:HEAD_DIM], axis=0, keepdims=True)
-        vw_ref[p, 1:2, :] = jnp.sum(both[HEAD_DIM:], axis=0, keepdims=True)
-        vw_ref[p, 2:3, :] = jnp.sum(x * after, axis=0, keepdims=True)
+        first, last = p * PAIR, p * PAIR + HEAD_DIM
+        vw_ref[p, 0:1, :] = jnp.sum(both[first : first + HEAD_DIM], axis=0, keepdims=True)
+        vw_ref[p, 1:2, :] = jnp.sum(both[last : last + HEAD_DIM], axis=0, keepdims=True)
+        vw_ref[p, 2:3, :] = w_sums[:, first : first + PAIR]
         vw_ref[p, 3:8, :] = jnp.zeros((5, STATE), f32)
+
+
+def finish_kernel(
+    sizes, heads, prod_ref, maps_ref, out_ref, gmaps_ref,
+    land, mland, sq, sq_land, nrm, nrm_land,
+    send, recv, msend, mrecv, qsend, qrecv, nsend, nrecv,
+):
+    dp, ctx, tp = sizes
+    replicas = dp * ctx
+    my_tp = lax.axis_index("tp")
+    my_ctx = lax.axis_index("ctx")
+    my_dp = lax.axis_index("dp")
+    me = my_dp * ctx + my_ctx
+
+    def replica(offset):
+        return lax.rem(me + offset, replicas)
+
+    def place(other):
+        return (other // ctx, lax.rem(other, ctx), my_tp)
+
+    def beside(offset):
+        return (my_dp, my_ctx, lax.rem(my_tp + offset, tp))
+
+    barrier = pltpu.get_barrier_semaphore()
+    for o in range(1, replicas):
+        pl.semaphore_signal(
+            barrier, inc=1, device_id=place(replica(o)), device_id_type=pl.DeviceIdType.MESH
+        )
+    for o in range(1, tp):
+        pl.semaphore_signal(
+            barrier, inc=1, device_id=beside(o), device_id_type=pl.DeviceIdType.MESH
+        )
+    pl.semaphore_wait(barrier, replicas - 1 + tp - 1)
+
+    def copy(src, dst, sends, recvs, o, to):
+        made = pltpu.make_async_remote_copy(
+            src_ref=src,
+            dst_ref=dst,
+            send_sem=sends.at[o - 1],
+            recv_sem=recvs.at[o - 1],
+            device_id=to,
+            device_id_type=pl.DeviceIdType.MESH,
+        )
+        made.start()
+        return made
+
+    big = []
+    for o in range(1, replicas):
+        other = replica(o)
+        big.append(copy(prod_ref.at[other], land.at[o - 1], send, recv, o, place(other)))
+    small = []
+    for o in range(1, tp):
+        target = lax.rem(my_tp + o, tp)
+        small.append(copy(maps_ref.at[target], mland.at[o - 1], msend, mrecv, o, beside(o)))
+    gmaps = maps_ref[my_tp].astype(f32)
+    for o in range(1, tp):
+        small[o - 1].wait_recv()
+        gmaps = gmaps + mland[o - 1].astype(f32)
+    gmaps_ref[...] = gmaps
+    total = prod_ref[me].astype(f32)
+    for o in range(1, replicas):
+        big[o - 1].wait_recv()
+        total = total + land[o - 1].astype(f32)
+    square = jnp.sum(total * total, axis=1, keepdims=True)
+    square = jnp.broadcast_to(square, sq.shape)
+    sq[...] = square
+    squares = [copy(sq, sq_land.at[o - 1], qsend, qrecv, o, beside(o)) for o in range(1, tp)]
+    for o in range(1, tp):
+        squares[o - 1].wait_recv()
+        square = square + sq_land[o - 1]
+    rows = out_ref.shape[0]
+    splits = total.shape[0] // rows
+    norm = square[:rows]
+    for k in range(1, splits):
+        norm = norm + square[k * rows : (k + 1) * rows]
+    norm = jnp.sqrt(norm + epsilon)
+    norm_sum = jnp.broadcast_to(jnp.sum(norm, axis=0, keepdims=True), nrm.shape)
+    nrm[...] = norm_sum
+    norms = [copy(nrm, nrm_land.at[o - 1], nsend, nrecv, o, place(replica(o))) for o in range(1, replicas)]
+    for o in range(1, replicas):
+        norms[o - 1].wait_recv()
+        norm_sum = norm_sum + nrm_land[o - 1]
+    scale = jnp.minimum(1.0, norm_sum[0:1] / heads / norm)[:, 0:1]
+    columns = total.shape[1]
+    for k in range(splits):
+        out_ref[:, k * columns : (k + 1) * columns] = total[k * rows : (k + 1) * rows] * scale
+    for made in big + small + squares + norms:
+        made.wait_send()
 
 
 def segments(lengths_row, anchor, length):
@@ -318,20 +407,57 @@
     step_grad = u_rows / steps + decay_rate[:, None] * tail_sum
     dt_grad = (step_grad * jax.nn.sigmoid(raw_steps)).astype(bf16)
 
-    tp = lax.axis_size("tp")
+    sizes = (lax.axis_size("dp"), count, lax.axis_size("tp"))
+    tp, replicas = sizes[2], sizes[0] * count
     maps = jnp.concatenate([local_b + bgrad, local_c], axis=1).astype(bf16)
-    maps = lax.all_to_all(maps.reshape(tp, length // tp, 2 * STATE), "tp", 0, 0)
-    grad_maps = jnp.sum(maps.astype(f32), axis=0)
-
+    maps = maps.reshape(tp, length // tp, 2 * STATE)
     gathered = lax.all_gather(dt_grad, "tp", axis=0, tiled=True)
-    replicas = lax.axis_size("dp") * count
-    product = jnp.dot(gathered, layer_in[0], preferred_element_type=f32).astype(bf16)
-    product = product.reshape(replicas, gathered.shape[0] // replicas, width)
-    summed = jnp.sum(lax.all_to_all(product, ("dp", "ctx"), 0, 0).astype(f32), axis=0)
-    squares = jnp.sum(summed * summed, axis=1)
-    own_norm = jnp.sqrt(lax.psum(squares, "tp") + epsilon)
-    target = jnp.sum(lax.all_gather(own_norm, ("dp", "ctx"))) / gathered.shape[0]
-    grad_dt_proj = summed * jnp.minimum(1.0, target / own_norm)[:, None]
+    rows = gathered.shape[0] // replicas
+    splits = max(16 // rows, 1)
+    columns = width // splits
+    product = jnp.concatenate(
+        [
+            jnp.dot(
+                gathered,
+                layer_in[0, :, k * columns : (k + 1) * columns],
+                preferred_element_type=f32,
+            ).astype(bf16).reshape(replicas, rows, columns)
+            for k in range(splits)
+        ],
+        axis=1,
+    )
+    piece = (splits * rows, columns)
+    vmem = pl.BlockSpec(memory_space=pltpu.VMEM)
+    sems = pltpu.SemaphoreType.DMA
+    grad_dt_proj, grad_maps = pl.pallas_call(
+        functools.partial(finish_kernel, sizes, gathered.shape[0]),
+        in_specs=[vmem, vmem],
+        out_specs=[vmem, vmem],
+        out_shape=[
+            jax.ShapeDtypeStruct((rows, width), f32),
+            jax.ShapeDtypeStruct((length // tp, 2 * STATE), f32),
+        ],
+        scratch_shapes=[
+            pltpu.VMEM((replicas - 1,) + piece, bf16),
+            pltpu.VMEM((tp - 1, length // tp, 2 * STATE), bf16),
+            pltpu.VMEM((piece[0], 128), f32),
+            pltpu.VMEM((tp - 1, piece[0], 128), f32),
+            pltpu.VMEM((8, 128), f32),
+            pltpu.VMEM((replicas - 1, 8, 128), f32),
+            sems((replicas - 1,)),
+            sems((replicas - 1,)),
+            sems((tp - 1,)),
+            sems((tp - 1,)),
+            sems((tp - 1,)),
+            sems((tp - 1,)),
+            sems((replicas - 1,)),
+            sems((replicas - 1,)),
+        ],
+        compiler_params=pltpu.CompilerParams(
+            collective_id=0, has_side_effects=True, vmem_limit_bytes=40 * 1024 * 1024
+        ),
+        name="finish",
+    )(product, maps)
     return (grad_x[None], grad_maps[None], grad_dt_proj)
 
 

time: 215 us -> 167 us (0.78)
  blocking collectives: 41.8 us -> 3.79 us
  Pallas kernels: 60.4 us -> 90.3 us
  waiting for transfers between devices: 31.9 us -> 5.86 us
  starting transfers between devices: 16.9 us -> 5.02 us
  other arithmetic: 15.1 us -> 12 us
  matrix products: 7.59 us -> 9.76 us
    pallas_call x0 -> x1, Pallas kernels: none -> 39.3 us  [shards(): pl.pallas_call(functools.partial(finish_kernel, sizes, gathered.shape[0])...]
    unnamed x1 -> x0, blocking collectives: 34.1 us -> none
    all_to_all x2 -> x0, waiting for transfers between devices: 26.1 us -> none  [the longest x1 22.4 us: shards(): lax.all_to_all(product, ('dp', 'ctx'), 0, 0).astype(f32)]
    all_to_all x2 -> x0, starting transfers between devices: 12.1 us -> none  [the longest x1 8.64 us: shards(): lax.all_to_all(product, ('dp', 'ctx'), 0, 0).astype(f32)]
    pallas_call x1, Pallas kernels: 16.4 us -> 9.02 us  [shards(): pl.pallas_call(functools.partial(enter_kernel, wide_pairs), grid=(groups,...]
    psum x1 -> x0, blocking collectives: 3.77 us -> none  [shards(): own_norm = jnp.sqrt(lax.psum(squares, 'tp') + epsilon)]
    unnamed x51 -> x41, local copies, waits for them, and re-layouts: 21.6 us -> 21.7 us
  transfers between devices with their start and end apart: 7 -> 5, of which waited for: 3 -> 1; matrix products, arithmetic and copies ran while one was open for 3% -> 4% of each run, Pallas kernels for 15% -> 18%
where the time goes in v2:
time: 167 us; the launch traced here: 165 us
  Pallas kernels  90.3 us (54%)
  local copies, waits for them, and re-layouts  36.9 us (22%)
  other arithmetic  12 us (7%)
  matrix products  9.76 us (6%)
  waiting for transfers between devices  5.86 us (4%)
  starting transfers between devices  5.02 us (3%)
  blocking collectives  3.79 us (2%)
  between operations  1.7 us (1%)
    pallas_call x1, Pallas kernels, shards(): pl.pallas_call(functools.partial(finish_kernel, sizes, gathered.shape[0])...  39.3 us
    pallas_call x4, Pallas kernels, shards(): pl.pallas_call(functools.partial(quad_kernel, quad_pairs), grid=(quad_gro...  30.1 us
    unnamed x41, local copies, waits for them, and re-layouts  21.7 us
    pallas_call x1, Pallas kernels, shards(): pl.pallas_call(functools.partial(leave_kernel, wide_pairs), grid=(groups,...  11.8 us
    pallas_call x1, Pallas kernels, shards(): pl.pallas_call(functools.partial(enter_kernel, wide_pairs), grid=(groups,...  9.02 us
    ppermute x2, waiting for transfers between devices, shift(): return jax.tree.map(lambda part: lax.ppermute(part, 'ctx', moves), value)  5.85 us
    dot_general x2, matrix products, shards(): jnp.dot(gathered, layer_in[0, :, k * columns:(k + 1) * columns], preferre...  4.15 us
    all_gather x1, blocking collectives, shards(): gathered = lax.all_gather(dt_grad, 'tp', axis=0, tiled=True)  3.79 us
  transfers between devices with their start and end apart: 5, of which 1 were waited for; matrix products, arithmetic and copies ran while one was open for 4% of the time, Pallas kernels for 18%

profile of v2, /device:TPU:1, one launch (start us, length us, event | category | flops | bytes accessed | tf_op | source)
XLA Modules:
  0.0 165.3 jit_solution(1966588763372988731)
XLA Ops:
  0.6 1.0 copy.106
  1.7 0.7 exponential_negate_fusion
  2.4 0.6 fusion.16
  2.9 0.1 copy.107
  3.1 0.2 slice_reduce_fusion
  3.3 1.0 reduce-window.8
  4.4 0.6 slice.34
  5.0 0.6 fusion.43
  6.2 0.7 compare_convert_fusion.2
  6.9 1.0 multiply_subtract_fusion
  7.9 0.1 copy.116
  8.1 1.1 copy.114
  9.2 0.1 copy.111
  9.4 0.1 copy.109
  9.6 0.2 maximum_bitcast_fusion
  9.9 0.4 reshape.101.aux_ref
  10.3 1.0 slice_bitcast_fusion
  11.3 2.2 %copy-done.2 = bf16[1,512,4096]{2,1,0:T(8,128)(2,1)S(1)} copy-done((bf16[1,512,4096]{2,1,0:T(8,128)(2,1)S(1)}, bf16[1,512,4096]{2,1,0:T(8,128)(2,1)}, u32[]{:S(2)}) %copy-start.2) | copy-done | bytes 4194328
  13.5 9.0 %enter.1 = (bf16[4096,128]{1,0:T(8,128)(2,1)S(1)}, f32[512,128]{1,0:T(8,128)S(1)}, f32[512,128]{1,0:T(8,128)S(1)}) custom-call(f32[32,8,512]{2,1,0:T(8,128)S(1)} %reshape.101.aux_ref, bf16[512,4096]{1,0:T(8,128)(2,1)S(1)} %bitcast.114, bf16[512,128]{1,0:T(8,128)(2,1)S(1)} %get-tuple-element.49.c_ref, f32[4096,128]{1,0:T(8,128)S(1)} %bitcast.112), custom_call_target="tpu_custom_call" | custom-call | tf_op jit(solution)/shard_map/enter/pallas_call | solution.py:291
  22.5 1.0 copy-done.8
  23.5 0.7 copy-done.9
  24.2 2.3 %reshape.103 = bf16[2,32,8192]{2,1,0:T(8,128)(2,1)} reshape(bf16[4096,128]{1,0:T(8,128)(2,1)} %copy-done.8) | data formatting | bytes 2097152 | tf_op jit(solution)/shard_map/reshape | solution.py:312
  26.5 1.9 %dynamic-slice_bitcast_fusion = bf16[32,8192]{1,0:T(8,128)(2,1)} fusion(bf16[2,32,8192]{2,1,0:T(8,128)(2,1)} %reshape.103, s32[]{:T(128)S(6)} %select_n.78), kind=kLoop, calls=%fused_computation.36 | loop fusion | bytes 1048580 | tf_op jit(solution)/shard_map/jit(dynamic_index_in_dim)/squeeze | solution.py:310
  28.4 2.0 %collective-permute-start = (bf16[32,8192]{1,0:T(8,128)(2,1)}, bf16[32,8192]{1,0:T(8,128)(2,1)}, u32[]{:S(2)}, u32[]{:S(2)}) collective-permute-start(bf16[32,8192]{1,0:T(8,128)(2,1)} %dynamic-slice_bitcast_fusion), channel_id=1, source_target_pairs={{0,2},{2,0},{4,6},{6,4},{8,10},{10,8},{12,14},{14,12},{1,3},{3,1},... | collective-permute-start | bytes 1572872 | tf_op jit(solution)/shard_map/ppermute | solution.py:315
  30.5 0.7 slice_reduce_fusion.3
  31.2 0.1 copy.121.labc_ref
  31.4 2.2 %copy-done.3 = bf16[1,512,4096]{2,1,0:T(8,128)(2,1)S(1)} copy-done((bf16[1,512,4096]{2,1,0:T(8,128)(2,1)S(1)}, bf16[1,512,4096]{2,1,0:T(8,128)(2,1)}, u32[]{:S(2)}) %copy-start.3) | copy-done | bytes 4194328
  33.6 2.2 %copy-done.5 = bf16[1,512,4096]{2,1,0:T(8,128)(2,1)S(1)} copy-done((bf16[1,512,4096]{2,1,0:T(8,128)(2,1)S(1)}, bf16[1,512,4096]{2,1,0:T(8,128)(2,1)}, u32[]{:S(2)}) %copy-start.5) | copy-done | bytes 4194328
  35.8 7.5 %quad.4 = (f32[512,4096]{1,0:T(8,128)}, f32[4,4,512]{2,1,0:T(4,128)S(1)}, f32[512,512]{1,0:T(8,128)S(1)}) custom-call(f32[32,8,512]{2,1,0:T(8,128)S(1)} %reshape.101.aux_ref, bf16[512,4096]{1,0:T(8,128)(2,1)S(1)} %bitcast.119, bf16[512,4096]{1,0:T(8,128)(2,1)S(1)} %bitcast.115, bf16[512,128]{1,0:T(8,128)(2,1)S(1)} %get-tuple-element.50.b_ref, ...), custom_call_target="tpu_custom_call" | custom-call | flops 12499999744 | bytes 5000000 | tf_op jit(solution)/shard_map/quad/pallas_call | solution.py:345
  43.3 1.0 copy-done.12
  44.3 1.4 fusion.13
  45.7 1.3 collective-permute-start.2
  47.1 2.2 %copy-done.4 = bf16[1,512,4096]{2,1,0:T(8,128)(2,1)S(1)} copy-done((bf16[1,512,4096]{2,1,0:T(8,128)(2,1)S(1)}, bf16[1,512,4096]{2,1,0:T(8,128)(2,1)}, u32[]{:S(2)}) %copy-start.4) | copy-done | bytes 4194328
  49.2 2.2 %copy-done.6 = bf16[1,512,4096]{2,1,0:T(8,128)(2,1)S(1)} copy-done((bf16[1,512,4096]{2,1,0:T(8,128)(2,1)S(1)}, bf16[1,512,4096]{2,1,0:T(8,128)(2,1)}, u32[]{:S(2)}) %copy-start.6) | copy-done | bytes 4194328
  51.4 1.2 copy-done.13
  52.6 7.6 %quad.5 = (f32[512,4096]{1,0:T(8,128)}, f32[4,4,512]{2,1,0:T(4,128)S(1)}, f32[512,512]{1,0:T(8,128)S(1)}) custom-call(f32[32,8,512]{2,1,0:T(8,128)S(1)} %reshape.101.aux_ref, bf16[512,4096]{1,0:T(8,128)(2,1)S(1)} %bitcast.120, bf16[512,4096]{1,0:T(8,128)(2,1)S(1)} %bitcast.116, ...), custom_call_target="tpu_custom_call", output_to_operand_aliasing={{0}: (8, {})} | custom-call | flops 12499999744 | bytes 5000000 | tf_op jit(solution)/shard_map/quad/pallas_call | solution.py:345
  60.2 0.2 add_convert_fusion
  60.4 1.5 collective-permute-start.3
  61.9 7.6 %quad.6 = (f32[512,4096]{1,0:T(8,128)}, f32[4,4,512]{2,1,0:T(4,128)S(1)}, f32[512,512]{1,0:T(8,128)S(1)}) custom-call(f32[32,8,512]{2,1,0:T(8,128)S(1)} %reshape.101.aux_ref, bf16[512,4096]{1,0:T(8,128)(2,1)S(1)} %bitcast.121, bf16[512,4096]{1,0:T(8,128)(2,1)S(1)} %bitcast.117, ...), custom_call_target="tpu_custom_call", output_to_operand_aliasing={{0}: (8, {})} | custom-call | flops 12499999744 | bytes 5000000 | tf_op jit(solution)/shard_map/quad/pallas_call | solution.py:345
  69.5 5.8 %collective-permute-done.3 = bf16[32,8192]{1,0:T(8,128)(2,1)S(1)} collective-permute-done((bf16[32,8192]{1,0:T(8,128)(2,1)S(1)}, bf16[32,8192]{1,0:T(8,128)(2,1)S(1)}, u32[]{:S(2)}, u32[]{:S(2)}) %collective-permute-start.3) | collective-permute-done | bytes 524320 | tf_op jit(solution)/shard_map/ppermute | solution.py:256
  75.3 2.3 %fusion.19 = (bf16[1,32,8192]{2,1,0:T(8,128)(2,1)}, bf16[32,8192]{1,0:T(8,128)(2,1)}) fusion(bf16[32,8192]{1,0:T(8,128)(2,1)S(1)} %collective-permute-done.3, f32[32]{0:T(128)S(1)} %get-tuple-element.55, pred[]{:T(512)S(6)} %eq.48, bf16[32,8192]{1,0:T(8,128)(2,1)} %collective-permute-done, bf16[2,32,8192]{2,1,0:T(8,128)(2,1)S(1)} %copy-done.14, s32[]{:T(128)S(6)} %select_n.79), kind=kLoop, calls=%fused_computation.32 | loop fusion | flops 2097152 | bytes 2621573 | tf_op jit(solution)/shard_map/stack | solution.py:333
  77.7 0.2 collective-permute-start.4
  77.9 7.5 %quad.7 = (f32[512,4096]{1,0:T(8,128)}, f32[4,4,512]{2,1,0:T(4,128)S(1)}, f32[512,512]{1,0:T(8,128)S(1)}) custom-call(f32[32,8,512]{2,1,0:T(8,128)S(1)} %reshape.101.aux_ref, bf16[512,4096]{1,0:T(8,128)(2,1)S(1)} %bitcast.122, bf16[512,4096]{1,0:T(8,128)(2,1)S(1)} %bitcast.118, ...), custom_call_target="tpu_custom_call", output_to_operand_aliasing={{0}: (8, {})} | custom-call | flops 12499999744 | bytes 5000000 | tf_op jit(solution)/shard_map/quad/pallas_call | solution.py:345
  85.4 1.1 copy-done.10
  86.4 0.8 copy.125
  87.3 0.8 copy.124
  88.1 0.8 copy.123
  89.0 0.8 copy.122
  89.8 2.4 %fusion.10 = bf16[512,128]{1,0:T(8,128)(2,1)} fusion(f32[512,128]{1,0:T(8,128)} %copy-done.9, bf16[1,512,256]{2,1,0:T(8,128)(2,1)} %param.10, f32[512,512]{1,0:T(8,128)} %copy-done.10, s32[512]{0:T(512)S(1)} %convert_reduce_fusion), kind=kOutput, calls=%fused_computation.17 | convolution fusion | flops 68288512 | bytes 1576960 | tf_op jit(solution)/shard_map/dot_general | solution.py:21
  92.3 2.7 %maximum_select_fusion = bf16[2,32,8192]{2,1,0:T(8,128)(2,1)} fusion(bf16[1,32,8192]{2,1,0:T(8,128)(2,1)} %bitcast.17, bf16[1,32,8192]{2,1,0:T(8,128)(2,1)} %get-tuple-element.45, pred[]{:T(512)S(6)} %eq.48), kind=kLoop, calls=%fused_computation.22 | loop fusion | flops 1572864 | bytes 2097153 | tf_op jit(solution)/shard_map/jit(_where)/select_n | solution.py:333
  95.0 2.3 %select_n.88.carry_ref = bf16[4096,128]{1,0:T(8,128)(2,1)} reshape(bf16[2,32,8192]{2,1,0:T(8,128)(2,1)} %maximum_select_fusion) | data formatting | bytes 2097152 | tf_op jit(solution)/shard_map/jit(_where)/select_n | solution.py:333
  97.3 1.2 copy-done.1
  98.6 2.2 %copy-done.7 = bf16[1,512,4096]{2,1,0:T(8,128)(2,1)S(1)} copy-done((bf16[1,512,4096]{2,1,0:T(8,128)(2,1)S(1)}, bf16[1,512,4096]{2,1,0:T(8,128)(2,1)}, u32[]{:S(2)}) %copy-start.7) | copy-done | bytes 4194328
  100.7 11.8 %leave.1 = (bf16[512,4096]{1,0:T(8,128)(2,1)}, f32[512,128]{1,0:T(8,128)S(1)}, f32[512,128]{1,0:T(8,128)S(1)}, f32[32,8,128]{2,1,0:T(8,128)S(1)}) custom-call(f32[32,8,512]{2,1,0:T(8,128)S(1)} %reshape.101.aux_ref, bf16[512,4096]{1,0:T(8,128)(2,1)S(1)} %bitcast.123, f32[512,4096]{1,0:T(8,128)} %get-tuple-element.30.r_ref, ...), custom_call_target="tpu_custom_call" | custom-call | tf_op jit(solution)/shard_map/leave/pallas_call | solution.py:383
  112.9 0.1 reduce_sum.44
  113.0 0.7 fusion.44
  113.7 2.3 %fusion.11 = bf16[64,512]{0,1:T(8,128)(2,1)S(1)} fusion(f32[16,512]{0,1:T(8,128)} %copy.125, f32[16,512]{0,1:T(8,128)} %copy.124, f32[16,512]{0,1:T(8,128)} %copy.123, f32[16,512]{0,1:T(8,128)} %copy.122, f32[1,64,512]{1,2,0:T(8,128)} %copy-done.16, f32[512,128]{1,0:T(8,128)S(1)} %get-tuple-element.38, f32[512,128]{1,0:T(8,128)S(1)} %get-tuple-element.33, ...), kind=kOutput, calls=%fused_computation.18 | convolution fusion | flops 202244096 | bytes 1115136 | tf_op jit(solution)/shard_map/dot_general | solution.py:465
  116.1 3.8 %all_gather.3 = bf16[128,512]{1,0:T(8,128)(2,1)S(1)} all-gather(bf16[64,512]{1,0:T(8,128)(2,1)S(1)} %copy.127), channel_id=1, replica_groups=mesh['dp'=2,'ctx'=8,'tp'=2] {'tp'}, dimensions={0}, use_global_device_ids=true | all-gather | bytes 196608 | tf_op jit(solution)/shard_map/all_gather | solution.py:414
  119.9 2.1 %fusion.1 = bf16[16,8,2048]{2,1,0:T(8,128)(2,1)S(1)} fusion(bf16[128,512]{1,0:T(8,128)(2,1)S(1)} %all_gather.3, bf16[1,512,4096]{2,1,0:T(8,128)(2,1)} %param.14), kind=kOutput, calls=%fused_computation.3 | convolution fusion | flops 268697600 | bytes 2752512 | tf_op jit(solution)/shard_map/dot_general | solution.py:420
  122.0 2.1 %fusion = bf16[16,8,2048]{2,1,0:T(8,128)(2,1)S(1)} fusion(bf16[128,512]{1,0:T(8,128)(2,1)S(1)} %all_gather.3, bf16[1,512,4096]{2,1,0:T(8,128)(2,1)} %param.14), kind=kOutput, calls=%fused_computation.2 | convolution fusion | flops 268697600 | bytes 2752512 | tf_op jit(solution)/shard_map/dot_general | solution.py:420
  124.1 0.4 fusion.9
  124.6 39.3 %finish.1 = (f32[8,4096]{1,0:T(8,128)S(1)}, f32[256,256]{1,0:T(8,128)S(1)}) custom-call(bf16[16,16,2048]{2,1,0:T(8,128)(2,1)S(1)} %pad_maximum_fusion.prod_ref, bf16[2,256,256]{2,1,0:T(8,128)(2,1)S(1)} %pad_maximum_fusion.1.maps_ref), custom_call_target="tpu_custom_call" | custom-call | tf_op jit(solution)/shard_map/finish/pallas_call | solution.py:432
  163.9 0.7 copy.134
  164.6 0.7 copy.135
  (52 shorter events, 1.2 us)
Async XLA Ops:
  1.7 8.2 %copy-start.16 = (f32[1,64,512]{1,2,0:T(8,128)}, f32[1,64,512]{1,2,0:T(8,128)S(1)}, u32[]{:S(2)}) copy-start(f32[1,64,512]{1,2,0:T(8,128)S(1)} %copy.106) | copy-start | bytes 393220
  2.9 8.4 %copy-start = (f32[1,1,64,64,128]{4,3,2,1,0:T(8,128)S(1)}, f32[1,1,64,64,128]{4,3,2,1,0:T(8,128)}, u32[]{:S(2)}) copy-start(f32[1,1,64,64,128]{4,3,2,1,0:T(8,128)} %param.13) | copy-start | bytes 6291460
  7.9 3.4 %copy-start.15 = (f32[64,512]{0,1:T(8,128)}, f32[64,512]{0,1:T(8,128)S(1)}, u32[]{:S(2)}) copy-start(f32[64,512]{0,1:T(8,128)S(1)} %get-tuple-element.52) | copy-start | bytes 393220
  11.3 2.2 %copy-start.2 = (bf16[1,512,4096]{2,1,0:T(8,128)(2,1)S(1)}, bf16[1,512,4096]{2,1,0:T(8,128)(2,1)}, u32[]{:S(2)}) copy-start(bf16[1,512,4096]{2,1,0:T(8,128)(2,1)} %param.9) | copy-start | bytes 12582916
  22.5 1.0 copy-start.8
  23.5 0.7 copy-start.9
  28.4 15.9 %collective-permute-start = (bf16[32,8192]{1,0:T(8,128)(2,1)}, bf16[32,8192]{1,0:T(8,128)(2,1)}, u32[]{:S(2)}, u32[]{:S(2)}) collective-permute-start(bf16[32,8192]{1,0:T(8,128)(2,1)} %dynamic-slice_bitcast_fusion), channel_id=1, source_target_pairs={{0,2},{2,0},{4,6},{6,4},{8,10},{10,8},{12,14},{14,12},{1,3},{3,1},... | collective-permute-start | bytes 1572872 | tf_op jit(solution)/shard_map/ppermute | solution.py:315
  31.2 13.0 %collective-permute-start.1 = (f32[32]{0:T(128)S(1)}, f32[32]{0:T(128)S(1)}, u32[]{:S(2)}, u32[]{:S(2)}) collective-permute-start(f32[32]{0:T(128)S(1)} %fusion.41), channel_id=1, source_target_pairs={{0,2},{2,0},{4,6},{6,4},{8,10},{10,8},{12,14},{14,12},{1,3},{3,1},... | collective-permute-start | bytes 392 | tf_op jit(solution)/shard_map/ppermute | solution.py:316
  31.4 2.2 %copy-start.3 = (bf16[1,512,4096]{2,1,0:T(8,128)(2,1)S(1)}, bf16[1,512,4096]{2,1,0:T(8,128)(2,1)}, u32[]{:S(2)}) copy-start(bf16[1,512,4096]{2,1,0:T(8,128)(2,1)} %param.9) | copy-start | bytes 12582916
  33.6 2.2 %copy-start.5 = (bf16[1,512,4096]{2,1,0:T(8,128)(2,1)S(1)}, bf16[1,512,4096]{2,1,0:T(8,128)(2,1)}, u32[]{:S(2)}) copy-start(bf16[1,512,4096]{2,1,0:T(8,128)(2,1)} %param.8) | copy-start | bytes 12582916
  43.3 1.0 copy-start.12
  45.7 14.5 %collective-permute-start.2 = (bf16[32,8192]{1,0:T(8,128)(2,1)S(1)}, bf16[32,8192]{1,0:T(8,128)(2,1)S(1)}, u32[]{:S(2)}, u32[]{:S(2)}) collective-permute-start(bf16[32,8192]{1,0:T(8,128)(2,1)S(1)} %fusion.13), channel_id=1, source_target_pairs={{4,0},{6,2},{8,4},{10,6},{12,8},{14,10},{5,1},{7,3},{9,5},{11,7},{... | collective-permute-start | bytes 1572872 | tf_op jit(solution)/shard_map/ppermute | solution.py:256
  47.0 2.2 %copy-start.4 = (bf16[1,512,4096]{2,1,0:T(8,128)(2,1)S(1)}, bf16[1,512,4096]{2,1,0:T(8,128)(2,1)}, u32[]{:S(2)}) copy-start(bf16[1,512,4096]{2,1,0:T(8,128)(2,1)} %param.9) | copy-start | bytes 12582916
  49.2 2.2 %copy-start.6 = (bf16[1,512,4096]{2,1,0:T(8,128)(2,1)S(1)}, bf16[1,512,4096]{2,1,0:T(8,128)(2,1)}, u32[]{:S(2)}) copy-start(bf16[1,512,4096]{2,1,0:T(8,128)(2,1)} %param.8) | copy-start | bytes 12582916
  51.4 1.2 copy-start.13
  60.4 14.9 %collective-permute-start.3 = (bf16[32,8192]{1,0:T(8,128)(2,1)S(1)}, bf16[32,8192]{1,0:T(8,128)(2,1)S(1)}, u32[]{:S(2)}, u32[]{:S(2)}) collective-permute-start(bf16[32,8192]{1,0:T(8,128)(2,1)S(1)} %add_convert_fusion), channel_id=1, source_target_pairs={{4,0},{6,2},{8,4},{10,6},{12,8},{14,10},{5,1},{7,3},{9,5},{11,7},{... | collective-permute-start | bytes 1572872 | tf_op jit(solution)/shard_map/ppermute | solution.py:256
  61.9 13.4 %copy-start.14 = (bf16[2,32,8192]{2,1,0:T(8,128)(2,1)S(1)}, bf16[2,32,8192]{2,1,0:T(8,128)(2,1)}, u32[]{:S(2)}) copy-start(bf16[2,32,8192]{2,1,0:T(8,128)(2,1)} %reshape.103) | copy-start | bytes 3145732
  77.7 14.6 %collective-permute-start.4 = (bf16[32,8192]{1,0:T(8,128)(2,1)}, bf16[32,8192]{1,0:T(8,128)(2,1)}, u32[]{:S(2)}, u32[]{:S(2)}) collective-permute-start(bf16[32,8192]{1,0:T(8,128)(2,1)} %get-tuple-element.46), channel_id=1, source_target_pairs={{0,2},{2,0},{4,6},{6,4},{8,10},{10,8},{12,14},{14,12},{1,3},{3,1},... | collective-permute-start | bytes 1572872 | tf_op jit(solution)/shard_map/ppermute | solution.py:331
  85.4 1.1 copy-start.10
  97.3 1.2 copy-start.1
  98.6 2.2 %copy-start.7 = (bf16[1,512,4096]{2,1,0:T(8,128)(2,1)S(1)}, bf16[1,512,4096]{2,1,0:T(8,128)(2,1)}, u32[]{:S(2)}) copy-start(bf16[1,512,4096]{2,1,0:T(8,128)(2,1)} %param.8) | copy-start | bytes 12582916
  113.7 10.4 %copy-start.11 = (f32[512,512]{1,0:T(8,128)S(1)}, f32[512,512]{1,0:T(8,128)}, u32[]{:S(2)}) copy-start(f32[512,512]{1,0:T(8,128)} %copy-done.10) | copy-start | bytes 3145732
  113.7 10.4 %copy-start.17 = (bf16[1,512,256]{2,1,0:T(8,128)(2,1)S(1)}, bf16[1,512,256]{2,1,0:T(8,128)(2,1)}, u32[]{:S(2)}) copy-start(bf16[1,512,256]{2,1,0:T(8,128)(2,1)} %param.10) | copy-start | bytes 786436
  119.9 4.6 %copy-start.18 = (bf16[512,128]{1,0:T(8,128)(2,1)S(1)}, bf16[512,128]{1,0:T(8,128)(2,1)}, u32[]{:S(2)}) copy-start(bf16[512,128]{1,0:T(8,128)(2,1)} %fusion.10) | copy-start | bytes 393220

commit v3 on v2

--- a/solution.py
+++ b/solution.py
@@ -287,7 +287,7 @@
     aux_spec = pl.BlockSpec((wide_pairs, 8, length), lambda g: (g, 0, 0))
     col_spec = pl.BlockSpec((length, wide_pairs * PAIR), lambda g: (0, g))
     row_spec = pl.BlockSpec((wide_pairs * PAIR, STATE), lambda g: (g, 0))
-    limit = pltpu.CompilerParams(vmem_limit_bytes=40 * 1024 * 1024)
+    limit = pltpu.CompilerParams(vmem_limit_bytes=56 * 1024 * 1024)
     local, state_term, enter_out = pl.pallas_call(
         functools.partial(enter_kernel, wide_pairs),
         grid=(groups,),
@@ -309,7 +309,7 @@
     def take(value, which):
         return lax.dynamic_index_in_dim(value, which, 0, keepdims=False)
 
-    whole_local = local.reshape(2, half, HEAD_DIM * STATE)
+    whole_local = local.reshape(2, half, HEAD_DIM, STATE)
     half_ends = ends.reshape(2, half)
     mine, mine_end = take(whole_local, odd), take(half_ends, odd)
     other = lax.ppermute(take(whole_local, 1 - odd), "ctx", swap)
@@ -317,17 +317,17 @@
     first = jnp.where(odd == 0, mine, other).astype(f32)
     second = jnp.where(odd == 0, other, mine).astype(f32)
     first_end = jnp.where(odd == 0, mine_end, other_end)
-    group = (first + first_end[:, None] * second).astype(bf16)
+    group = (first + first_end[:, None, None] * second).astype(bf16)
     group_end = mine_end * other_end
     reach, window = 1, max(count // 4, 1)
     while reach < window:
         ahead, ahead_end = shift((group, group_end), 2 * reach, count)
-        group = (group.astype(f32) + group_end[:, None] * ahead.astype(f32)).astype(bf16)
+        group = (group.astype(f32) + group_end[:, None, None] * ahead.astype(f32)).astype(bf16)
         group_end = group_end * ahead_end
         reach *= 2
     after = shift(group, 2, count)
     even_end = jnp.where(odd == 0, other_end, mine_end)
-    even_after = (second + even_end[:, None] * after.astype(f32)).astype(bf16)
+    even_after = (second + even_end[:, None, None] * after.astype(f32)).astype(bf16)
     back = lax.ppermute(jnp.where(odd == 0, after, even_after), "ctx", swap)
     kept = jnp.where(odd == 0, even_after, after)
     carry = jnp.where(odd == 0, jnp.stack([kept, back]), jnp.stack([back, kept]))

time: 167 us -> 146 us (0.87)
  local copies, waits for them, and re-layouts: 36.9 us -> 10.6 us
  Pallas kernels: 90.3 us -> 100 us
  other arithmetic: 12 us -> 6.69 us
    unnamed x41 -> x23, local copies, waits for them, and re-layouts: 21.7 us -> 2.42 us
    pallas_call x4, Pallas kernels: 30.1 us -> 37.2 us  [shards(): pl.pallas_call(functools.partial(quad_kernel, quad_pairs), grid=(quad_gro...]
    select_n x1 -> x0, local copies, waits for them, and re-layouts: 2.34 us -> none  [shards(): jnp.where(odd == 0, jnp.stack([kept, back]), jnp.stack([back, kept]))]
    reshape x1 -> x0, local copies, waits for them, and re-layouts: 2.33 us -> none  [shards(): whole_local = local.reshape(2, half, HEAD_DIM * STATE)]
    reshape x8, local copies, waits for them, and re-layouts: 3.41 us -> 1.31 us  [shards(): a_parts.append(a_part.reshape(-1, length))]
    pallas_call x1, Pallas kernels: 9.02 us -> 11 us  [shards(): pl.pallas_call(functools.partial(enter_kernel, wide_pairs), grid=(groups,...]
    another operation x1, other arithmetic: 2.33 us -> 0.44 us  [shards(): jnp.stack([kept, back])]
  transfers between devices with their start and end apart: 5 -> 5, of which waited for: 1 -> 3; matrix products, arithmetic and copies ran while one was open for 4% -> 3% of each run, Pallas kernels for 18% -> 26%
where the time goes in v3:
time: 146 us; the launch traced here: 144 us
  Pallas kernels  100 us (68%)
  local copies, waits for them, and re-layouts  10.6 us (7%)
  matrix products  8.65 us (6%)
  waiting for transfers between devices  7.14 us (5%)
  other arithmetic  6.69 us (5%)
  starting transfers between devices  5.47 us (4%)
  blocking collectives  3.92 us (3%)
  between operations  1.72 us (1%)
    pallas_call x1, Pallas kernels, shards(): pl.pallas_call(functools.partial(finish_kernel, sizes, gathered.shape[0])...  39.1 us
    pallas_call x4, Pallas kernels, shards(): pl.pallas_call(functools.partial(quad_kernel, quad_pairs), grid=(quad_gro...  37.2 us
    pallas_call x1, Pallas kernels, shards(): pl.pallas_call(functools.partial(leave_kernel, wide_pairs), grid=(groups,...  12.9 us
    pallas_call x1, Pallas kernels, shards(): pl.pallas_call(functools.partial(enter_kernel, wide_pairs), grid=(groups,...  11 us
    ppermute x2, waiting for transfers between devices, shift(): return jax.tree.map(lambda part: lax.ppermute(part, 'ctx', moves), value)  5.52 us
    dot_general x2, matrix products, shards(): jnp.dot(gathered, layer_in[0, :, k * columns:(k + 1) * columns], preferre...  4.07 us
    all_gather x1, blocking collectives, shards(): gathered = lax.all_gather(dt_grad, 'tp', axis=0, tiled=True)  3.92 us
  transfers between devices with their start and end apart: 5, of which 3 were waited for; matrix products, arithmetic and copies ran while one was open for 3% of the time, Pallas kernels for 26%

profile of v3, /device:TPU:1, one launch (start us, length us, event | category | flops | bytes accessed | tf_op | source)
XLA Modules:
  0.0 144.5 jit_solution(14099970588870900308)
XLA Ops:
  0.6 1.0 copy.106
  1.7 0.7 exponential_negate_fusion
  2.3 0.5 fusion.16
  2.9 0.1 copy.107
  3.0 0.2 slice_reduce_fusion
  3.2 0.8 reduce-window.8
  4.1 0.1 convert_reduce_fusion
  4.2 0.6 slice.34
  4.7 0.6 fusion.43
  6.0 0.7 compare_convert_fusion.2
  6.7 0.3 multiply_subtract_fusion
  6.9 0.1 copy.116
  7.1 0.1 stack.32
  7.1 0.1 copy.114
  7.3 0.1 stack.31
  7.3 0.1 copy.111
  7.5 0.1 stack.30
  7.5 0.1 copy.109
  7.7 0.1 stack.29
  7.7 0.2 maximum_bitcast_fusion
  8.0 0.1 copy.117
  8.0 1.2 reshape.101.aux_ref
  9.2 0.7 slice_bitcast_fusion
  9.9 11.0 %enter.1 = (bf16[4096,128]{1,0:T(8,128)(2,1)}, f32[512,128]{1,0:T(8,128)}, f32[512,128]{1,0:T(8,128)}) custom-call(f32[32,8,512]{2,1,0:T(8,128)} %reshape.101.aux_ref, bf16[512,4096]{1,0:T(8,128)(2,1)} %bitcast.118, bf16[512,128]{1,0:T(8,128)(2,1)} %get-tuple-element.49.c_ref, f32[4096,128]{1,0:T(8,128)} %bitcast.115), custom_call_target="tpu_custom_call" | custom-call | tf_op jit(solution)/shard_map/enter/pallas_call | solution.py:291
  21.0 1.1 dynamic-slice_bitcast_fusion
  22.0 2.1 %collective-permute-start = (bf16[32,64,128]{2,1,0:T(8,128)(2,1)S(1)}, bf16[32,64,128]{2,1,0:T(8,128)(2,1)S(1)}, u32[]{:S(2)}, u32[]{:S(2)}) collective-permute-start(bf16[32,64,128]{2,1,0:T(8,128)(2,1)S(1)} %dynamic-slice_bitcast_fusion), channel_id=1, source_target_pairs={{0,2},{2,0},{4,6},{6,4},{8,10},{10,8},{12,14},{14,12},{1,3},{3,1},... | collective-permute-start | bytes 1572872 | tf_op jit(solution)/shard_map/ppermute | solution.py:315
  24.2 0.1 reshape_squeeze.6
  24.3 0.9 copy.121.labc_ref
  25.2 9.0 %quad.4 = (f32[512,4096]{1,0:T(8,128)}, f32[4,4,512]{2,1,0:T(4,128)}, f32[512,512]{1,0:T(8,128)}) custom-call(f32[32,8,512]{2,1,0:T(8,128)} %reshape.101.aux_ref, bf16[512,4096]{1,0:T(8,128)(2,1)} %bitcast.123, bf16[512,4096]{1,0:T(8,128)(2,1)} %bitcast.119, bf16[512,128]{1,0:T(8,128)(2,1)} %get-tuple-element.50.b_ref, ...), custom_call_target="tpu_custom_call" | custom-call | flops 12499999744 | bytes 5000000 | tf_op jit(solution)/shard_map/quad/pallas_call | solution.py:345
  34.2 1.6 %collective-permute-done.1 = f32[32]{0:T(128)S(1)} collective-permute-done((f32[32]{0:T(128)S(1)}, f32[32]{0:T(128)S(1)}, u32[]{:S(2)}, u32[]{:S(2)}) %collective-permute-start.1) | collective-permute-done | bytes 160 | tf_op jit(solution)/shard_map/ppermute | solution.py:316
  35.8 0.3 fusion.13
  36.1 1.3 collective-permute-start.2
  37.4 9.4 %quad.5 = (f32[512,4096]{1,0:T(8,128)}, f32[4,4,512]{2,1,0:T(4,128)}, f32[512,512]{1,0:T(8,128)}) custom-call(f32[32,8,512]{2,1,0:T(8,128)} %reshape.101.aux_ref, bf16[512,4096]{1,0:T(8,128)(2,1)} %bitcast.124, bf16[512,4096]{1,0:T(8,128)(2,1)} %bitcast.120, bf16[512,128]{1,0:T(8,128)(2,1)} %get-tuple-element.50.b_ref, ...), custom_call_target="tpu_custom_call", output_to_operand_aliasing={{0}: (8, {})} | custom-call | flops 12499999744 | bytes 5000000 | tf_op jit(solution)/shard_map/quad/pallas_call | solution.py:345
  46.8 3.3 %collective-permute-done.2 = bf16[32,64,128]{2,1,0:T(8,128)(2,1)S(1)} collective-permute-done((bf16[32,64,128]{2,1,0:T(8,128)(2,1)S(1)}, bf16[32,64,128]{2,1,0:T(8,128)(2,1)S(1)}, u32[]{:S(2)}, u32[]{:S(2)}) %collective-permute-start.2) | collective-permute-done | bytes 524320 | tf_op jit(solution)/shard_map/ppermute | solution.py:256
  50.1 0.2 add_convert_fusion
  50.4 1.5 %collective-permute-start.3 = (bf16[32,64,128]{2,1,0:T(8,128)(2,1)S(1)}, bf16[32,64,128]{2,1,0:T(8,128)(2,1)S(1)}, u32[]{:S(2)}, u32[]{:S(2)}) collective-permute-start(bf16[32,64,128]{2,1,0:T(8,128)(2,1)S(1)} %add_convert_fusion), channel_id=1, source_target_pairs={{4,0},{6,2},{8,4},{10,6},{12,8},{14,10},{5,1},{7,3},{9,5},{11,7},{... | collective-permute-start | bytes 1572872 | tf_op jit(solution)/shard_map/ppermute | solution.py:256
  51.8 9.4 %quad.6 = (f32[512,4096]{1,0:T(8,128)}, f32[4,4,512]{2,1,0:T(4,128)}, f32[512,512]{1,0:T(8,128)}) custom-call(f32[32,8,512]{2,1,0:T(8,128)} %reshape.101.aux_ref, bf16[512,4096]{1,0:T(8,128)(2,1)} %bitcast.125, bf16[512,4096]{1,0:T(8,128)(2,1)} %bitcast.121, bf16[512,128]{1,0:T(8,128)(2,1)} %get-tuple-element.50.b_ref, ...), custom_call_target="tpu_custom_call", output_to_operand_aliasing={{0}: (8, {})} | custom-call | flops 12499999744 | bytes 5000000 | tf_op jit(solution)/shard_map/quad/pallas_call | solution.py:345
  61.2 2.2 %collective-permute-done.3 = bf16[32,64,128]{2,1,0:T(8,128)(2,1)S(1)} collective-permute-done((bf16[32,64,128]{2,1,0:T(8,128)(2,1)S(1)}, bf16[32,64,128]{2,1,0:T(8,128)(2,1)S(1)}, u32[]{:S(2)}, u32[]{:S(2)}) %collective-permute-start.3) | collective-permute-done | bytes 524320 | tf_op jit(solution)/shard_map/ppermute | solution.py:256
  63.4 0.4 fusion.19
  63.9 0.6 collective-permute-start.4
  64.5 9.4 %quad.7 = (f32[512,4096]{1,0:T(8,128)}, f32[4,4,512]{2,1,0:T(4,128)}, f32[512,512]{1,0:T(8,128)}) custom-call(f32[32,8,512]{2,1,0:T(8,128)} %reshape.101.aux_ref, bf16[512,4096]{1,0:T(8,128)(2,1)} %bitcast.126, bf16[512,4096]{1,0:T(8,128)(2,1)} %bitcast.122, bf16[512,128]{1,0:T(8,128)(2,1)} %get-tuple-element.50.b_ref, ...), custom_call_target="tpu_custom_call", output_to_operand_aliasing={{0}: (8, {})} | custom-call | flops 12499999744 | bytes 5000000 | tf_op jit(solution)/shard_map/quad/pallas_call | solution.py:345
  73.9 0.8 reshape.107
  74.7 0.1 copy.125
  74.8 0.1 copy.124
  75.0 0.1 copy.123
  75.2 0.1 copy.122
  75.3 1.7 %fusion.10 = bf16[512,128]{1,0:T(8,128)(2,1)S(1)} fusion(f32[512,128]{1,0:T(8,128)} %get-tuple-element.42, bf16[1,512,256]{2,1,0:T(8,128)(2,1)S(1)} %copy-done.1, f32[512,512]{1,0:T(8,128)} %get-tuple-element.40, s32[512]{0:T(512)S(1)} %copy-done.6), kind=kOutput, calls=%fused_computation.17 | convolution fusion | flops 68288512 | bytes 1576960 | tf_op jit(solution)/shard_map/dot_general | solution.py:21
  77.0 1.1 maximum_select_fusion
  78.1 12.9 %leave.1 = (bf16[512,4096]{1,0:T(8,128)(2,1)}, f32[512,128]{1,0:T(8,128)}, f32[512,128]{1,0:T(8,128)}, f32[32,8,128]{2,1,0:T(8,128)}) custom-call(f32[32,8,512]{2,1,0:T(8,128)} %reshape.101.aux_ref, bf16[512,4096]{1,0:T(8,128)(2,1)} %bitcast.127, f32[512,4096]{1,0:T(8,128)} %get-tuple-element.30.r_ref, bf16[512,128]{1,0:T(8,128)(2,1)} %get-tuple-element.50.b_ref, ...), custom_call_target="tpu_custom_call" | custom-call | tf_op jit(solution)/shard_map/leave/pallas_call | solution.py:383
  91.1 1.0 slice_reduce_fusion.2
  92.0 1.0 slice_reduce_fusion.1
  93.0 0.1 reshape_squeeze.7
  93.1 0.1 reshape.108
  93.2 0.1 reduce_sum.44
  93.4 2.0 %fusion.11 = bf16[64,512]{0,1:T(8,128)(2,1)S(1)} fusion(f32[16,512]{0,1:T(8,128)S(1)} %copy.125, f32[16,512]{0,1:T(8,128)S(1)} %copy.124, f32[16,512]{0,1:T(8,128)S(1)} %copy.123, f32[16,512]{0,1:T(8,128)S(1)} %copy.122, f32[1,64,512]{1,2,0:T(8,128)S(1)} %copy.106, f32[512,128]{1,0:T(8,128)S(1)} %copy-done.7, f32[512,128]{1,0:T(8,128)} %get-tuple-element.33, ...), kind=kOutput, calls=%fused_computation.18 | convolution fusion | flops 202244096 | bytes 1114624 | tf_op jit(solution)/shard_map/dot_general | solution.py:465
  95.4 0.1 copy.127
  95.5 3.9 %all_gather.3 = bf16[128,512]{1,0:T(8,128)(2,1)S(1)} all-gather(bf16[64,512]{1,0:T(8,128)(2,1)S(1)} %copy.127), channel_id=1, replica_groups=mesh['dp'=2,'ctx'=8,'tp'=2] {'tp'}, dimensions={0}, use_global_device_ids=true | all-gather | bytes 196608 | tf_op jit(solution)/shard_map/all_gather | solution.py:414
  99.4 2.0 %fusion.1 = bf16[16,8,2048]{2,1,0:T(8,128)(2,1)S(1)} fusion(bf16[128,512]{1,0:T(8,128)(2,1)S(1)} %all_gather.3, bf16[1,512,4096]{2,1,0:T(8,128)(2,1)} %param.14), kind=kOutput, calls=%fused_computation.3 | convolution fusion | flops 268697600 | bytes 2752512 | tf_op jit(solution)/shard_map/dot_general | solution.py:420
  101.4 2.0 %fusion = bf16[16,8,2048]{2,1,0:T(8,128)(2,1)S(1)} fusion(bf16[128,512]{1,0:T(8,128)(2,1)S(1)} %all_gather.3, bf16[1,512,4096]{2,1,0:T(8,128)(2,1)} %param.14), kind=kOutput, calls=%fused_computation.2 | convolution fusion | flops 268697600 | bytes 2752512 | tf_op jit(solution)/shard_map/dot_general | solution.py:420
  103.5 0.3 fusion.9
  103.9 0.1 pad_maximum_fusion.prod_ref
  104.0 39.1 %finish.1 = (f32[8,4096]{1,0:T(8,128)S(1)}, f32[256,256]{1,0:T(8,128)S(1)}) custom-call(bf16[16,16,2048]{2,1,0:T(8,128)(2,1)S(1)} %pad_maximum_fusion.prod_ref, bf16[2,256,256]{2,1,0:T(8,128)(2,1)S(1)} %pad_maximum_fusion.1.maps_ref), custom_call_target="tpu_custom_call" | custom-call | tf_op jit(solution)/shard_map/finish/pallas_call | solution.py:432
  143.1 0.7 copy.134
  143.8 0.7 copy.135
  (32 shorter events, 0.2 us)
Async XLA Ops:
  2.3 6.9 %copy-start.1 = (bf16[1,512,256]{2,1,0:T(8,128)(2,1)S(1)}, bf16[1,512,256]{2,1,0:T(8,128)(2,1)}, u32[]{:S(2)}) copy-start(bf16[1,512,256]{2,1,0:T(8,128)(2,1)} %param.10) | copy-start | bytes 786436
  4.1 20.1 %copy-start.5 = (s32[512]{0:T(512)}, s32[512]{0:T(512)S(1)}, u32[]{:S(2)}) copy-start(s32[512]{0:T(512)S(1)} %convert_reduce_fusion) | copy-start | bytes 6148
  22.0 13.8 %collective-permute-start = (bf16[32,64,128]{2,1,0:T(8,128)(2,1)S(1)}, bf16[32,64,128]{2,1,0:T(8,128)(2,1)S(1)}, u32[]{:S(2)}, u32[]{:S(2)}) collective-permute-start(bf16[32,64,128]{2,1,0:T(8,128)(2,1)S(1)} %dynamic-slice_bitcast_fusion), channel_id=1, source_target_pairs={{0,2},{2,0},{4,6},{6,4},{8,10},{10,8},{12,14},{14,12},{1,3},{3,1},... | collective-permute-start | bytes 1572872 | tf_op jit(solution)/shard_map/ppermute | solution.py:315
  24.3 11.5 %collective-permute-start.1 = (f32[32]{0:T(128)S(1)}, f32[32]{0:T(128)S(1)}, u32[]{:S(2)}, u32[]{:S(2)}) collective-permute-start(f32[32]{0:T(128)S(1)} %fusion.41), channel_id=1, source_target_pairs={{0,2},{2,0},{4,6},{6,4},{8,10},{10,8},{12,14},{14,12},{1,3},{3,1},... | collective-permute-start | bytes 392 | tf_op jit(solution)/shard_map/ppermute | solution.py:316
  25.2 10.7 %copy-start = (bf16[4096,128]{1,0:T(8,128)(2,1)S(1)}, bf16[4096,128]{1,0:T(8,128)(2,1)}, u32[]{:S(2)}) copy-start(bf16[4096,128]{1,0:T(8,128)(2,1)} %get-tuple-element.31) | copy-start | bytes 3145732
  36.1 14.0 %collective-permute-start.2 = (bf16[32,64,128]{2,1,0:T(8,128)(2,1)S(1)}, bf16[32,64,128]{2,1,0:T(8,128)(2,1)S(1)}, u32[]{:S(2)}, u32[]{:S(2)}) collective-permute-start(bf16[32,64,128]{2,1,0:T(8,128)(2,1)S(1)} %fusion.13), channel_id=1, source_target_pairs={{4,0},{6,2},{8,4},{10,6},{12,8},{14,10},{5,1},{7,3},{9,5},{11,7},{... | collective-permute-start | bytes 1572872 | tf_op jit(solution)/shard_map/ppermute | solution.py:256
  50.4 13.1 %collective-permute-start.3 = (bf16[32,64,128]{2,1,0:T(8,128)(2,1)S(1)}, bf16[32,64,128]{2,1,0:T(8,128)(2,1)S(1)}, u32[]{:S(2)}, u32[]{:S(2)}) collective-permute-start(bf16[32,64,128]{2,1,0:T(8,128)(2,1)S(1)} %add_convert_fusion), channel_id=1, source_target_pairs={{4,0},{6,2},{8,4},{10,6},{12,8},{14,10},{5,1},{7,3},{9,5},{11,7},{... | collective-permute-start | bytes 1572872 | tf_op jit(solution)/shard_map/ppermute | solution.py:256
  63.9 13.1 %collective-permute-start.4 = (bf16[32,64,128]{2,1,0:T(8,128)(2,1)S(1)}, bf16[32,64,128]{2,1,0:T(8,128)(2,1)S(1)}, u32[]{:S(2)}, u32[]{:S(2)}) collective-permute-start(bf16[32,64,128]{2,1,0:T(8,128)(2,1)S(1)} %get-tuple-element.46), channel_id=1, source_target_pairs={{0,2},{2,0},{4,6},{6,4},{8,10},{10,8},{12,14},{14,12},{1,3},{3,1},... | collective-permute-start | bytes 1572872 | tf_op jit(solution)/shard_map/ppermute | solution.py:331
  64.5 10.3 %copy-start.4 = (f32[4,4,512]{2,1,0:T(4,128)S(1)}, f32[4,4,512]{2,1,0:T(4,128)}, u32[]{:S(2)}) copy-start(f32[4,4,512]{2,1,0:T(4,128)} %get-tuple-element.36) | copy-start | bytes 98308
  64.5 10.5 %copy-start.3 = (f32[4,4,512]{2,1,0:T(4,128)S(1)}, f32[4,4,512]{2,1,0:T(4,128)}, u32[]{:S(2)}) copy-start(f32[4,4,512]{2,1,0:T(4,128)} %get-tuple-element.35) | copy-start | bytes 98308
  64.5 10.6 %copy-start.2 = (f32[4,4,512]{2,1,0:T(4,128)S(1)}, f32[4,4,512]{2,1,0:T(4,128)}, u32[]{:S(2)}) copy-start(f32[4,4,512]{2,1,0:T(4,128)} %get-tuple-element.34) | copy-start | bytes 98308
  64.5 10.8 %copy-start.6 = (s32[512]{0:T(512)S(1)}, s32[512]{0:T(512)}, u32[]{:S(2)}) copy-start(s32[512]{0:T(512)} %copy-done.5) | copy-start | bytes 6148
  78.1 15.2 %copy-start.7 = (f32[512,128]{1,0:T(8,128)S(1)}, f32[512,128]{1,0:T(8,128)}, u32[]{:S(2)}) copy-start(f32[512,128]{1,0:T(8,128)} %get-tuple-element.38) | copy-start | bytes 786436
  93.4 10.1 %copy-start.8 = (f32[512,128]{1,0:T(8,128)S(1)}, f32[512,128]{1,0:T(8,128)}, u32[]{:S(2)}) copy-start(f32[512,128]{1,0:T(8,128)} %get-tuple-element.41) | copy-start | bytes 786436
  95.4 8.1 %copy-start.9 = (f32[512,512]{1,0:T(8,128)S(1)}, f32[512,512]{1,0:T(8,128)}, u32[]{:S(2)}) copy-start(f32[512,512]{1,0:T(8,128)} %get-tuple-element.40) | copy-start | bytes 3145732
